TPU v7x, 256 devices: a whole 4x4x8 slice. The times are simulated.
256 devices in a mesh: lev: 8 (over x_lo, y), tile: 32 (over x_hi, z, core).
Axes of the slice: x: 4 (x_hi: 2, x_lo: 2; x = x_hi * 2 + x_lo), y: 4, z: 8, core: 2. Of those that a mesh axis runs over, the one named last changes fastest.
Arguments:
- cotangent: bfloat16 [72, 96, 32768], P('lev', None, 'tile'), may hold values from -6 to 6
- particles: bfloat16 [72, 96, 32768], P('lev', None, 'tile'), may hold values from 0.049804688 to 2
- coag_rate: float32 [72], P('lev'), may hold values from 0.004 to 0.015
- courant: float32 [2, 72, 32768], P(None, 'lev', 'tile'), may hold values from 0.05 to 0.45
- offsets: int32 [2, 32768], P(None, 'tile'), may hold values from -2 to 2
- mass_flux: bfloat16 [72, 72, 32768], P(None, None, ('tile', 'lev')), may hold values from -0.75 to 0.75
- cloud_top: int32 [32768], P(('tile', 'lev')), may hold values from 18 to 71
Outputs:
- result: float32 [72, 96, 32768], P(None, None, ('tile', 'lev'))
All inputs are finite; a program needn't handle non-finite values.
Results may differ from a plain program's by a relative error of at most 0.0029.
Values may be sent and summed in bfloat16 or wider, within the bound.
No kernel may reach another device: no remote copies, remote signals or barrier semaphores. Data moves between devices by JAX's collectives and lax.ppermute only.
A program may use at most 64 MiB of HBM per device.

v0:
```python
import math

import jax
import jax.numpy as jnp
from jax import lax
from jax.sharding import PartitionSpec as P

NX = 128
REACH = 2


def extended(cells, sides, width):
    for axis, dim in sides:
        count = lax.axis_size(axis)
        ends = count - 1
        head = lax.slice_in_dim(cells, 0, width, axis=dim)
        tail = lax.slice_in_dim(cells, cells.shape[dim] - width, cells.shape[dim], axis=dim)
        cells = jnp.concatenate(
            [
                lax.ppermute(tail, axis, [(i, (i + 1) % count) for i in range(ends)]),
                cells,
                lax.ppermute(head, axis, [((i + 1) % count, i) for i in range(ends)]),
            ],
            axis=dim,
        )
    return cells


def make_tables(bins, freq_count):
    length = 2 * bins
    bin_index = lax.broadcasted_iota(jnp.int32, (freq_count, bins), 1)
    freq_index = lax.broadcasted_iota(jnp.int32, (freq_count, bins), 0)
    phase_angle = (bin_index * freq_index % length).astype(jnp.float32) * (2.0 * math.pi / length)
    kept_freq = freq_index >= 0
    weight = jnp.ones((freq_count, bins), jnp.float32)
    forward_table = jnp.concatenate(
        [
            jnp.where(kept_freq, jnp.cos(phase_angle), 0.0),
            jnp.where(kept_freq, -jnp.sin(phase_angle), 0.0),
        ],
        axis=0,
    ).astype(jnp.bfloat16)
    inverse_cos = (jnp.transpose(weight * jnp.cos(phase_angle)) / length).astype(jnp.bfloat16)
    inverse_sin = (jnp.transpose(-weight * jnp.sin(phase_angle)) / length).astype(jnp.bfloat16)
    return (forward_table, inverse_cos, inverse_sin)


def coagulate(gradients, amounts, coag_rate, tables, freq_count):
    forward_table, inverse_cos, inverse_sin = tables

    def one_level(pieces):
        gradient, particles, coefficient = pieces
        grad_spec = jnp.dot(forward_table, gradient, preferred_element_type=jnp.float32)
        mass_spec = jnp.dot(forward_table, particles, preferred_element_type=jnp.float32)
        grad_re = grad_spec[:freq_count]
        grad_im = grad_spec[freq_count:]
        mass_re = mass_spec[:freq_count]
        mass_im = mass_spec[freq_count:]
        prod_re = (mass_re * grad_re + mass_im * grad_im).astype(jnp.bfloat16)
        prod_im = (mass_re * grad_im - mass_im * grad_re).astype(jnp.bfloat16)
        correlation = jnp.dot(inverse_cos, prod_re, preferred_element_type=jnp.float32) + jnp.dot(
            inverse_sin, prod_im, preferred_element_type=jnp.float32
        )
        grad_wide = gradient.astype(jnp.float32)
        mass_wide = particles.astype(jnp.float32)
        total_mass = jnp.sum(mass_wide, axis=0)
        inner = jnp.sum(grad_wide * mass_wide, axis=0)
        return grad_wide + coefficient * (correlation - grad_wide * total_mass - inner)

    return lax.map(one_level, (gradients, amounts, coag_rate))


def body(cotangent, particles, coag_rate, courant, offsets, mass_flux, cloud_top):
    level_count, bins, cell_count = cotangent.shape
    row_count = cell_count // NX
    freq_count = 2 * bins
    tables = make_tables(bins, freq_count)
    adjoint = coagulate(cotangent, particles, coag_rate, tables, freq_count)
    adjoint = extended(adjoint.reshape(level_count, bins, row_count, NX), (("tile", 2),), REACH)
    centre_rows = adjoint[:, :, REACH : REACH + row_count, :]
    cour_y = courant[0].reshape(level_count, 1, row_count, NX)
    cour_x = courant[1].reshape(level_count, 1, row_count, NX)
    shift_y = offsets[0].reshape(row_count, NX)
    shift_x = offsets[1].reshape(row_count, NX)
    pad_x = jnp.pad(centre_rows, ((0, 0), (0, 0), (0, 0), (REACH, REACH)))
    along_y = jnp.zeros_like(centre_rows)
    along_x = jnp.zeros_like(centre_rows)
    for upwind in range(-REACH, REACH + 1):
        along_y = along_y + jnp.where(
            shift_y == upwind, adjoint[:, :, REACH + upwind : REACH + upwind + row_count, :], 0.0
        )
        along_x = along_x + jnp.where(
            shift_x == upwind, pad_x[:, :, :, REACH + upwind : REACH + upwind + NX], 0.0
        )
    remapped = centre_rows * (1.0 - cour_y - cour_x) + cour_y * along_y + cour_x * along_x
    remapped = remapped.astype(jnp.bfloat16).reshape(level_count, bins, cell_count)
    all_levels = mass_flux.shape[0]
    level_ids = lax.broadcasted_iota(jnp.int32, (all_levels, cloud_top.shape[0]), 0)
    inside = level_ids <= cloud_top[None, :]
    masked = jnp.where(
        inside[:, None, :] & inside[None, :, :], mass_flux, jnp.zeros_like(mass_flux)
    )
    received = lax.all_to_all(remapped, "lev", split_axis=2, concat_axis=0, tiled=True)
    mixing = jnp.einsum("obc,oic->ibc", received, masked, preferred_element_type=jnp.float32)
    return received.astype(jnp.float32) + mixing


def solution(mesh):
    placed = (
        P("lev", None, "tile"),
        P("lev", None, "tile"),
        P("lev"),
        P(None, "lev", "tile"),
        P(None, "tile"),
        P(None, None, ("tile", "lev")),
        P(("tile", "lev")),
    )
    return jax.shard_map(
        body, mesh=mesh, in_specs=placed, out_specs=P(None, None, ("tile", "lev")), check_vma=False
    )
```

profile of v0, /device:TPU:6, one launch (start us, length us, event | category | flops | bytes accessed | tf_op | source)
XLA Modules:
  0.0 171.8 jit_solution(14030658634548506464)
XLA Ops:
  0.5 72.2 %while.11 = (s32[]{:T(128)}, f32[9,96,1024]{2,1,0:T(8,128)}, bf16[9,96,1024]{2,1,0:T(8,128)(2,1)}, f32[9]{0:T(128)}, bf16[9,96,1024]{2,1,0:T(8,128)(2,1)}, /*index=5*/bf16[384,96]{1,0:T(8,128)(2,1)S(1)}, s32[]{:T(128)}) while((s32[]{:T(128)}, f32[9,96,1024]{2,1,0:T(8,128)}, bf16[9,96,1024]{2,1,0:T(8,128)(2,1)}, f32[9]{0:T(128)}, ...), condition=%wide.region_3.4_spmd.clone, body=%wide.region_0.3_spmd.clone.sunk | while | flops 229648384 | bytes 11766025 | solution.py:70
  5.5 3.0 %fusion.83 = f32[9,96,1024]{2,1,0:T(8,128)} fusion(f32[9,96,1024]{2,1,0:T(8,128)} %get-tuple-element.142, s32[]{:T(128)} %get-tuple-element.141, f32[1024,96]{0,1:T(8,128)S(1)} %fusion.82, f32[384,1024]{1,0:T(8,128)S(1)} %convolution_bitcast_fusion.4, f32[384,1024]{1,0:T(8,128)S(1)} %convolution_bitcast_fusion.5, f32[1024]{0:T(1024)S(1)} %get-tuple-element.132, ...), kind=kOutput, calls=%fused_computation.11.clone.1 | convolution fusion | flops 39426048 | bytes 4137984 | tf_op jit(solution)/shard_map/while/body/eval_jaxpr/dot_general | solution.py:61
  13.5 3.0 %fusion.83 = f32[9,96,1024]{2,1,0:T(8,128)} fusion(f32[9,96,1024]{2,1,0:T(8,128)} %get-tuple-element.142, s32[]{:T(128)} %get-tuple-element.141, f32[1024,96]{0,1:T(8,128)S(1)} %fusion.82, f32[384,1024]{1,0:T(8,128)S(1)} %convolution_bitcast_fusion.4, f32[384,1024]{1,0:T(8,128)S(1)} %convolution_bitcast_fusion.5, f32[1024]{0:T(1024)S(1)} %get-tuple-element.132, ...), kind=kOutput, calls=%fused_computation.11.clone.1 | convolution fusion | flops 39426048 | bytes 4137984 | tf_op jit(solution)/shard_map/while/body/eval_jaxpr/dot_general | solution.py:61
  21.5 3.0 %fusion.83 = f32[9,96,1024]{2,1,0:T(8,128)} fusion(f32[9,96,1024]{2,1,0:T(8,128)} %get-tuple-element.142, s32[]{:T(128)} %get-tuple-element.141, f32[1024,96]{0,1:T(8,128)S(1)} %fusion.82, f32[384,1024]{1,0:T(8,128)S(1)} %convolution_bitcast_fusion.4, f32[384,1024]{1,0:T(8,128)S(1)} %convolution_bitcast_fusion.5, f32[1024]{0:T(1024)S(1)} %get-tuple-element.132, ...), kind=kOutput, calls=%fused_computation.11.clone.1 | convolution fusion | flops 39426048 | bytes 4137984 | tf_op jit(solution)/shard_map/while/body/eval_jaxpr/dot_general | solution.py:61
  29.6 3.0 %fusion.83 = f32[9,96,1024]{2,1,0:T(8,128)} fusion(f32[9,96,1024]{2,1,0:T(8,128)} %get-tuple-element.142, s32[]{:T(128)} %get-tuple-element.141, f32[1024,96]{0,1:T(8,128)S(1)} %fusion.82, f32[384,1024]{1,0:T(8,128)S(1)} %convolution_bitcast_fusion.4, f32[384,1024]{1,0:T(8,128)S(1)} %convolution_bitcast_fusion.5, f32[1024]{0:T(1024)S(1)} %get-tuple-element.132, ...), kind=kOutput, calls=%fused_computation.11.clone.1 | convolution fusion | flops 39426048 | bytes 4137984 | tf_op jit(solution)/shard_map/while/body/eval_jaxpr/dot_general | solution.py:61
  37.6 3.0 %fusion.83 = f32[9,96,1024]{2,1,0:T(8,128)} fusion(f32[9,96,1024]{2,1,0:T(8,128)} %get-tuple-element.142, s32[]{:T(128)} %get-tuple-element.141, f32[1024,96]{0,1:T(8,128)S(1)} %fusion.82, f32[384,1024]{1,0:T(8,128)S(1)} %convolution_bitcast_fusion.4, f32[384,1024]{1,0:T(8,128)S(1)} %convolution_bitcast_fusion.5, f32[1024]{0:T(1024)S(1)} %get-tuple-element.132, ...), kind=kOutput, calls=%fused_computation.11.clone.1 | convolution fusion | flops 39426048 | bytes 4137984 | tf_op jit(solution)/shard_map/while/body/eval_jaxpr/dot_general | solution.py:61
  45.6 3.0 %fusion.83 = f32[9,96,1024]{2,1,0:T(8,128)} fusion(f32[9,96,1024]{2,1,0:T(8,128)} %get-tuple-element.142, s32[]{:T(128)} %get-tuple-element.141, f32[1024,96]{0,1:T(8,128)S(1)} %fusion.82, f32[384,1024]{1,0:T(8,128)S(1)} %convolution_bitcast_fusion.4, f32[384,1024]{1,0:T(8,128)S(1)} %convolution_bitcast_fusion.5, f32[1024]{0:T(1024)S(1)} %get-tuple-element.132, ...), kind=kOutput, calls=%fused_computation.11.clone.1 | convolution fusion | flops 39426048 | bytes 4137984 | tf_op jit(solution)/shard_map/while/body/eval_jaxpr/dot_general | solution.py:61
  53.6 3.0 %fusion.83 = f32[9,96,1024]{2,1,0:T(8,128)} fusion(f32[9,96,1024]{2,1,0:T(8,128)} %get-tuple-element.142, s32[]{:T(128)} %get-tuple-element.141, f32[1024,96]{0,1:T(8,128)S(1)} %fusion.82, f32[384,1024]{1,0:T(8,128)S(1)} %convolution_bitcast_fusion.4, f32[384,1024]{1,0:T(8,128)S(1)} %convolution_bitcast_fusion.5, f32[1024]{0:T(1024)S(1)} %get-tuple-element.132, ...), kind=kOutput, calls=%fused_computation.11.clone.1 | convolution fusion | flops 39426048 | bytes 4137984 | tf_op jit(solution)/shard_map/while/body/eval_jaxpr/dot_general | solution.py:61
  61.7 3.0 %fusion.83 = f32[9,96,1024]{2,1,0:T(8,128)} fusion(f32[9,96,1024]{2,1,0:T(8,128)} %get-tuple-element.142, s32[]{:T(128)} %get-tuple-element.141, f32[1024,96]{0,1:T(8,128)S(1)} %fusion.82, f32[384,1024]{1,0:T(8,128)S(1)} %convolution_bitcast_fusion.4, f32[384,1024]{1,0:T(8,128)S(1)} %convolution_bitcast_fusion.5, f32[1024]{0:T(1024)S(1)} %get-tuple-element.132, ...), kind=kOutput, calls=%fused_computation.11.clone.1 | convolution fusion | flops 39426048 | bytes 4137984 | tf_op jit(solution)/shard_map/while/body/eval_jaxpr/dot_general | solution.py:61
  69.7 3.0 %fusion.83 = f32[9,96,1024]{2,1,0:T(8,128)} fusion(f32[9,96,1024]{2,1,0:T(8,128)} %get-tuple-element.142, s32[]{:T(128)} %get-tuple-element.141, f32[1024,96]{0,1:T(8,128)S(1)} %fusion.82, f32[384,1024]{1,0:T(8,128)S(1)} %convolution_bitcast_fusion.4, f32[384,1024]{1,0:T(8,128)S(1)} %convolution_bitcast_fusion.5, f32[1024]{0:T(1024)S(1)} %get-tuple-element.132, ...), kind=kOutput, calls=%fused_computation.11.clone.1 | convolution fusion | flops 39426048 | bytes 4137984 | tf_op jit(solution)/shard_map/while/body/eval_jaxpr/dot_general | solution.py:61
  72.7 2.8 %copy.77 = f32[108,8,8,128]{3,2,1,0:T(8,128)S(1)} copy(f32[108,8,8,128]{3,1,2,0:T(8,128)} %bitcast.27) | data formatting | bytes 7077888
  78.4 8.1 %collective-permute-start.1 = (f32[9,96,2,128]{3,1,2,0:T(8,128)S(1)}, f32[9,96,2,128]{3,1,2,0:T(8,128)S(1)}, u32[]{:S(2)}, u32[]{:S(2)}) collective-permute-start(f32[9,96,2,128]{3,1,2,0:T(8,128)S(1)} %copy.66), channel_id=1, source_target_pairs={{1,0},{2,1},{3,2},{4,3},{5,4},{6,5},{7,6},{8,7},{9,8},{10,9},{11,1... | collective-permute-start | bytes 2654216 | tf_op jit(solution)/shard_map/ppermute | solution.py:22
  87.5 7.6 %collective-permute-done = f32[9,96,2,128]{3,1,2,0:T(8,128)S(1)} collective-permute-done((f32[9,96,2,128]{3,1,2,0:T(8,128)S(1)}, f32[9,96,2,128]{3,1,2,0:T(8,128)S(1)}, u32[]{:S(2)}, u32[]{:S(2)}) %collective-permute-start) | collective-permute-done | bytes 884768 | tf_op jit(solution)/shard_map/ppermute | solution.py:20
  98.0 6.1 %fusion.49 = bf16[9,96,8,128]{3,2,1,0:T(8,128)(2,1)S(1)} fusion(f32[9,96,2,128]{3,2,1,0:T(2,128)S(1)} %copy.65, f32[9,96,8,128]{3,2,1,0:T(8,128)S(1)} %bitcast.90, f32[9,96,10,128]{3,2,1,0:T(8,128)S(1)} %copy_dynamic-update-slice_fusion, f32[9,8,128]{2,1,0:T(8,128)S(1)} %bitcast.97, f32[9,8,128]{2,1,0:T(8,128)S(1)} %bitcast.95, ...), kind=kLoop, calls=%fused_computation.63 | loop fusion | flops 23003136 | bytes 13391872 | tf_op jit(solution)/shard_map/convert_element_type | solution.py:96
  104.1 4.7 %copy.74 = bf16[9,96,8,128]{1,0,3,2:T(8,128)(2,1)} copy(bf16[9,96,8,128]{3,2,1,0:T(8,128)(2,1)S(1)} %fusion.49) | data formatting | bytes 3538944 | tf_op jit(solution)/shard_map/reshape | solution.py:96
  108.8 8.0 %reshape.88 = bf16[8,2,55296]{2,1,0:T(2,128)(2,1)} reshape(bf16[1024,9,96]{2,1,0:T(8,128)(2,1)} %bitcast.91) | data formatting | bytes 3538944
  116.8 5.9 %all-to-all-start = ((bf16[8,2,55296]{2,1,0:T(2,128)(2,1)}), bf16[8,2,55296]{2,1,0:T(2,128)(2,1)S(1)}, u32[]{:S(2)}, u32[]{:S(2)}) async-start(bf16[8,2,55296]{2,1,0:T(2,128)(2,1)} %reshape.88), calls=%async_computation | async-start | bytes 3538944 | tf_op jit(solution)/shard_map/all_to_all | solution.py:103
  127.3 15.6 %all-to-all-done = bf16[8,2,55296]{2,1,0:T(2,128)(2,1)S(1)} async-done(((bf16[8,2,55296]{2,1,0:T(2,128)(2,1)}), bf16[8,2,55296]{2,1,0:T(2,128)(2,1)S(1)}, u32[]{:S(2)}, u32[]{:S(2)}) %all-to-all-start) | async-done | bytes 1769504 | tf_op jit(solution)/shard_map/all_to_all | solution.py:103
  142.9 6.2 %reshape.89 = bf16[1024,9,96]{2,1,0:T(8,128)(2,1)} reshape(bf16[8,2,55296]{2,1,0:T(2,128)(2,1)S(1)} %all-to-all-done) | data formatting | bytes 3538944
  149.1 4.1 %copy.70 = bf16[8,9,96,128]{3,2,1,0:T(8,128)(2,1)S(1)} copy(bf16[8,9,96,128]{2,1,3,0:T(8,128)(2,1)} %bitcast.92) | data formatting | bytes 3538944 | tf_op jit(solution)/shard_map/all_to_all | solution.py:103
  153.2 2.7 %copy.72 = bf16[72,96,128]{1,0,2:T(8,128)(2,1)} copy(bf16[72,96,128]{2,1,0:T(8,128)(2,1)S(1)} %bitcast.93) | data formatting | bytes 3538944 | tf_op jit(solution)/shard_map/all_to_all | solution.py:103
  156.0 5.9 %fusion.67 = f32[128,72,96]{2,1,0:T(8,128)} fusion(bf16[72,72,128]{0,1,2:T(8,128)(2,1)} %copy.71, bf16[72,96,128]{1,0,2:T(8,128)(2,1)} %copy.72), kind=kOutput, calls=%fused_computation.105 | convolution fusion | flops 127401984 | bytes 6635520 | tf_op jit(solution)/shard_map/obc,oic->ibc/dot_general | solution.py:104
  161.9 5.7 %copy.73 = f32[128,72,96]{0,2,1:T(8,128)} copy(f32[128,72,96]{2,1,0:T(8,128)} %fusion.67) | data formatting | bytes 7077888 | tf_op jit(solution)/shard_map/obc,oic->ibc/dot_general | solution.py:104
  167.5 4.3 %bitcast_add_fusion = f32[72,96,128]{2,1,0:T(8,128)} fusion(f32[128,72,96]{0,2,1:T(8,128)} %copy.73, bf16[8,9,96,128]{3,2,1,0:T(8,128)(2,1)S(1)} %copy.70), kind=kLoop, calls=%fused_computation.77 | loop fusion | flops 1769472 | bytes 8847360 | tf_op jit(solution)/shard_map/add | solution.py:105
  (86 shorter events, 56.5 us)
Async XLA Ops:
  0.5 4.3 %copy-start.3 = (f32[9]{0:T(128)S(1)}, f32[9]{0:T(128)}, u32[]{:S(2)}) copy-start(f32[9]{0:T(128)} %get-tuple-element.151) | copy-start | bytes 112 | tf_op jit(solution)/shard_map/while
  8.5 4.3 %copy-start.3 = (f32[9]{0:T(128)S(1)}, f32[9]{0:T(128)}, u32[]{:S(2)}) copy-start(f32[9]{0:T(128)} %get-tuple-element.151) | copy-start | bytes 112 | tf_op jit(solution)/shard_map/while
  16.5 4.3 %copy-start.3 = (f32[9]{0:T(128)S(1)}, f32[9]{0:T(128)}, u32[]{:S(2)}) copy-start(f32[9]{0:T(128)} %get-tuple-element.151) | copy-start | bytes 112 | tf_op jit(solution)/shard_map/while
  24.6 4.3 %copy-start.3 = (f32[9]{0:T(128)S(1)}, f32[9]{0:T(128)}, u32[]{:S(2)}) copy-start(f32[9]{0:T(128)} %get-tuple-element.151) | copy-start | bytes 112 | tf_op jit(solution)/shard_map/while
  32.6 4.3 %copy-start.3 = (f32[9]{0:T(128)S(1)}, f32[9]{0:T(128)}, u32[]{:S(2)}) copy-start(f32[9]{0:T(128)} %get-tuple-element.151) | copy-start | bytes 112 | tf_op jit(solution)/shard_map/while
  40.6 4.3 %copy-start.3 = (f32[9]{0:T(128)S(1)}, f32[9]{0:T(128)}, u32[]{:S(2)}) copy-start(f32[9]{0:T(128)} %get-tuple-element.151) | copy-start | bytes 112 | tf_op jit(solution)/shard_map/while
  48.6 4.3 %copy-start.3 = (f32[9]{0:T(128)S(1)}, f32[9]{0:T(128)}, u32[]{:S(2)}) copy-start(f32[9]{0:T(128)} %get-tuple-element.151) | copy-start | bytes 112 | tf_op jit(solution)/shard_map/while
  56.7 4.3 %copy-start.3 = (f32[9]{0:T(128)S(1)}, f32[9]{0:T(128)}, u32[]{:S(2)}) copy-start(f32[9]{0:T(128)} %get-tuple-element.151) | copy-start | bytes 112 | tf_op jit(solution)/shard_map/while
  64.7 4.3 %copy-start.3 = (f32[9]{0:T(128)S(1)}, f32[9]{0:T(128)}, u32[]{:S(2)}) copy-start(f32[9]{0:T(128)} %get-tuple-element.151) | copy-start | bytes 112 | tf_op jit(solution)/shard_map/while
  75.6 10.9 %copy-start.1 = (s32[2,1024]{1,0:T(2,128)S(1)}, s32[2,1024]{1,0:T(2,128)}, u32[]{:S(2)}) copy-start(s32[2,1024]{1,0:T(2,128)} %param.13) | copy-start | bytes 24580
  76.3 18.8 %collective-permute-start = (f32[9,96,2,128]{3,1,2,0:T(8,128)S(1)}, f32[9,96,2,128]{3,1,2,0:T(8,128)S(1)}, u32[]{:S(2)}, u32[]{:S(2)}) collective-permute-start(f32[9,96,2,128]{3,1,2,0:T(8,128)S(1)} %copy.64), channel_id=1, source_target_pairs={{0,1},{1,2},{2,3},{3,4},{4,5},{5,6},{6,7},{7,8},{8,9},{9,10},{10,1... | collective-permute-start | bytes 2654216 | tf_op jit(solution)/shard_map/ppermute | solution.py:20
  78.4 18.6 %collective-permute-start.1 = (f32[9,96,2,128]{3,1,2,0:T(8,128)S(1)}, f32[9,96,2,128]{3,1,2,0:T(8,128)S(1)}, u32[]{:S(2)}, u32[]{:S(2)}) collective-permute-start(f32[9,96,2,128]{3,1,2,0:T(8,128)S(1)} %copy.66), channel_id=1, source_target_pairs={{1,0},{2,1},{3,2},{4,3},{5,4},{6,5},{7,6},{8,7},{9,8},{10,9},{11,1... | collective-permute-start | bytes 2654216 | tf_op jit(solution)/shard_map/ppermute | solution.py:22
  86.6 0.9 copy-start
  108.8 14.0 %copy-start.2 = (s32[128]{0:T(128)S(1)}, s32[128]{0:T(128)}, u32[]{:S(2)}) copy-start(s32[128]{0:T(128)} %param.15) | copy-start | bytes 1540
  116.8 26.1 %all-to-all-start = ((bf16[8,2,55296]{2,1,0:T(2,128)(2,1)}), bf16[8,2,55296]{2,1,0:T(2,128)(2,1)S(1)}, u32[]{:S(2)}, u32[]{:S(2)}) async-start(bf16[8,2,55296]{2,1,0:T(2,128)(2,1)} %reshape.88), calls=%async_computation | async-start | bytes 3538944 | tf_op jit(solution)/shard_map/all_to_all | solution.py:103
where the time goes:
time: 173 us; the launch traced here: 172 us
  matrix products  61.8 us (36%)
  local copies, waits for them, and re-layouts  46.5 us (27%)
  waiting for transfers between devices  24.4 us (14%)
  other arithmetic  22.9 us (13%)
  starting transfers between devices  15.9 us (9%)
    dot_general x9, matrix products, one_level(): jnp.dot(inverse_sin, prod_im, preferred_element_type=jnp.float32)  27.2 us
    unnamed x10, local copies, waits for them, and re-layouts  17.9 us
    all_to_all x1, waiting for transfers between devices, body(): lax.all_to_all(remapped, 'lev', split_axis=2, concat_axis=0, tiled=True)  15.6 us
    dot_general x9, matrix products, one_level(): jnp.dot(forward_table, gradient, preferred_element_type=jnp.float32)  11.6 us
    dot_general x9, matrix products, one_level(): jnp.dot(forward_table, particles, preferred_element_type=jnp.float32)  11.5 us
    reduce_sum x9, other arithmetic, one_level(): total_mass = jnp.sum(mass_wide, axis=0)  10 us
    ppermute x1, starting transfers between devices, extended(): lax.ppermute(head, axis, [((i + 1) % count, i) for i in range(ends)])  8.05 us
    ppermute x1, waiting for transfers between devices, extended(): lax.ppermute(tail, axis, [(i, (i + 1) % count) for i in range(ends)])  7.59 us
  transfers between devices with their start and end apart: 3, of which 3 were waited for; matrix products, arithmetic and copies ran while one was open for 3% of the time, Pallas kernels for 0%

commit v1 on v0

v1 whole, which is shorter than its diff:
```python
import functools
import math

import jax
import jax.numpy as jnp
import ml_dtypes
import numpy as np
from jax import lax
from jax.experimental import pallas as pl
from jax.experimental.pallas import tpu as pltpu
from jax.sharding import PartitionSpec as P

NX = 128
ROWS = 8
REACH = 2
BINS = 96
LOCAL = 9
LEVELS = 72
PEERS = 8
STEP = 3
SUB = 4
MIX = 12
BF16 = jnp.bfloat16
F32 = jnp.float32


def tables():
    length = 2 * BINS
    freq, bins = np.arange(BINS)[:, None], np.arange(BINS)[None, :]
    theta = 2.0 * math.pi * ((freq * bins) % length) / length
    nyquist = 1.0 - 2.0 * (np.arange(BINS) % 2)
    cos, sin = np.cos(theta), -np.sin(theta)
    sin[0] = nyquist
    forward = np.concatenate([cos, sin], axis=0)
    weight = np.where(np.arange(BINS) == 0, 1.0, 2.0)[:, None] / length
    inverse = np.concatenate([cos * weight, sin * weight], axis=0).T
    return forward.astype(ml_dtypes.bfloat16), np.ascontiguousarray(inverse).astype(ml_dtypes.bfloat16)


def adjoint_of(forward, inverse, gradient, amounts, coefficient):
    grad_spec = jnp.dot(forward, gradient, preferred_element_type=F32)
    mass_spec = jnp.dot(forward, amounts, preferred_element_type=F32)
    grad_re, grad_im = grad_spec[:BINS], grad_spec[BINS:]
    mass_re, mass_im = mass_spec[:BINS], mass_spec[BINS:]
    total_mass = mass_re[0:1]
    first = lax.broadcasted_iota(jnp.int32, (8, gradient.shape[1]), 0) == 0
    re_re, im_im = mass_re * grad_re, mass_im * grad_im
    prod_re = re_re + im_im
    prod_im = mass_re * grad_im - mass_im * grad_re
    prod_re = jnp.concatenate([jnp.where(first, re_re[:8], prod_re[:8]), prod_re[8:]], axis=0)
    prod_im = jnp.concatenate([jnp.where(first, im_im[:8], prod_im[:8]), prod_im[8:]], axis=0)
    prod = jnp.concatenate([prod_re.astype(BF16), prod_im.astype(BF16)], axis=0)
    correlation = jnp.dot(inverse, prod, preferred_element_type=F32)
    grad_wide = gradient.astype(F32)
    inner = jnp.sum(grad_wide * amounts.astype(F32), axis=0, keepdims=True)
    return grad_wide + coefficient * (correlation - grad_wide * total_mass - inner)


def edge_kernel(rate, forward, inverse, grad_lo, mass_lo, grad_hi, mass_hi, wide, lo, hi):
    step = pl.program_id(0)

    def level(j, carry):
        coefficient = rate[step * STEP + j]
        for side, (grad, mass, out) in enumerate(((grad_lo, mass_lo, lo), (grad_hi, mass_hi, hi))):
            adjoint = adjoint_of(forward[...], inverse[...], grad[j], mass[j], coefficient)
            wide[j, :, side * 256 : (side + 1) * 256] = adjoint
            out[j] = adjoint.astype(BF16)
        return carry

    lax.fori_loop(0, STEP, level, 0)


def inner_kernel(rate, forward, inverse, grad_lo, mass_lo, grad_hi, mass_hi, wide, courant, offsets, ready, partial, cells):
    step = pl.program_id(0)
    lane = lax.broadcasted_iota(jnp.int32, (1, NX), 1)

    def level(j, carry):
        coefficient = rate[step * STEP + j]
        cells[:, 0:256] = wide[j, :, 0:256]
        cells[:, 768:1024] = wide[j, :, 256:512]
        for side, (grad, mass) in enumerate(((grad_lo, mass_lo), (grad_hi, mass_hi))):
            adjoint = adjoint_of(forward[...], inverse[...], grad[j], mass[j], coefficient)
            cells[:, (side + 1) * 256 : (side + 2) * 256] = adjoint
        for row in range(ROWS):
            span = slice(row * NX, (row + 1) * NX)
            cour_y, cour_x = courant[j, 0:1, span], courant[j, 1:2, span]
            shift_y, shift_x = offsets[0:1, span], offsets[1:2, span]
            centre = cells[:, span]
            total = centre * (1.0 - cour_y - cour_x)
            for upwind in range(-REACH, REACH + 1):
                if 0 <= row + upwind < ROWS:
                    weight = jnp.where(shift_y == upwind, cour_y, 0.0)
                    near = slice((row + upwind) * NX, (row + upwind + 1) * NX)
                    total = total + cells[:, near] * weight
            place = lane + shift_x
            weight = jnp.where((place >= 0) & (place < NX), cour_x, 0.0)
            place = jnp.broadcast_to(jnp.clip(place, 0, NX - 1), centre.shape)
            along_x = jnp.take_along_axis(centre, place, axis=1, mode="promise_in_bounds")
            total = total + along_x * weight
            if 2 <= row < 6:
                ready[row - 2, j] = total.astype(BF16)
            else:
                partial[row if row < 2 else row - 4, j] = total
        return carry

    lax.fori_loop(0, STEP, level, 0)


def finish_kernel(me, ready, partial, above, below, courant, offsets, *outs):
    def level(j, carry):
        for turn in range(PEERS):
            row = jnp.bitwise_xor(me[0], turn)
            out = outs[turn]

            @pl.when((row >= 2) & (row < 6))
            def _():
                out[j] = ready[row - 2, j]

            for edge, (place, terms) in enumerate(
                (
                    (0, ((above, 0, -2), (above, 1, -1))),
                    (1, ((above, 1, -2),)),
                    (6, ((below, 0, 2),)),
                    (7, ((below, 0, 1), (below, 1, 2))),
                )
            ):

                @pl.when(row == place)
                def _(edge=edge, place=place, terms=terms):
                    span = slice(place * NX, (place + 1) * NX)
                    cour_y, shift_y = courant[j, 0:1, span], offsets[0:1, span]
                    total = partial[edge, j]
                    for ref, line, upwind in terms:
                        weight = jnp.where(shift_y == upwind, cour_y, 0.0)
                        total = total + ref[j, :, line * NX : (line + 1) * NX].astype(F32) * weight
                    out[j] = total.astype(BF16)

        return carry

    lax.fori_loop(0, STEP, level, 0)


def mix_kernel(has_acc, source, flux, cloud_top, block, *refs):
    acc = refs[0] if has_acc else None
    out, weights, wide = refs[-3:]
    step = pl.program_id(0)

    @pl.when(step == 0)
    def _():
        top = cloud_top[...]
        levels = lax.broadcasted_iota(jnp.int32, (LEVELS, NX), 0)
        inside = levels <= top
        for o in range(LOCAL):
            level = source[0] * LOCAL + o
            kept = jnp.where(inside & (level <= top), flux[o].astype(F32), 0.0)
            weights[o] = kept + jnp.where(levels == level, 1.0, 0.0)
            wide[o] = block[o].astype(F32)

    def some(q, carry):
        first = step * MIX + q * SUB
        sums = [acc[q * SUB + n] if has_acc else None for n in range(SUB)]
        for o in range(LOCAL):
            data = wide[o]
            for n in range(SUB):
                term = data * weights[o, pl.ds(first + n, 1), :]
                sums[n] = term if sums[n] is None else sums[n] + term
        for n in range(SUB):
            out[q * SUB + n] = sums[n]
        return carry

    lax.fori_loop(0, MIX // SUB, some, 0)


def mix(source, flux, cloud_top, block, acc):
    has_acc = acc is not None
    rows = pl.BlockSpec((MIX, BINS, NX), lambda i, s: (i, 0, 0))
    in_specs = [
        pl.BlockSpec((LOCAL, LEVELS, NX), lambda i, s: (s[0], 0, 0)),
        pl.BlockSpec((1, NX), lambda i, s: (0, 0)),
        pl.BlockSpec((LOCAL, BINS, NX), lambda i, s: (0, 0, 0)),
    ]
    return pl.pallas_call(
        functools.partial(mix_kernel, has_acc),
        out_shape=jax.ShapeDtypeStruct((LEVELS, BINS, NX), F32),
        grid_spec=pltpu.PrefetchScalarGridSpec(
            num_scalar_prefetch=1,
            grid=(LEVELS // MIX,),
            in_specs=in_specs + ([rows] if has_acc else []),
            out_specs=rows,
            scratch_shapes=[pltpu.VMEM((LOCAL, LEVELS, NX), F32), pltpu.VMEM((LOCAL, BINS, NX), F32)],
        ),
        input_output_aliases={4: 0} if has_acc else {},
        compiler_params=pltpu.CompilerParams(vmem_limit_bytes=24 << 20),
        cost_estimate=pl.CostEstimate(flops=4_000_000, bytes_accessed=7_000_000, transcendentals=0),
        name="mix",
    )(source, flux, cloud_top, block, *([acc] if has_acc else []))


def whole(shape):
    return pl.BlockSpec(shape, lambda i: (0,) * len(shape))


def body(cotangent, particles, coag_rate, courant, offsets, mass_flux, cloud_top):
    forward, inverse = (jnp.asarray(t) for t in tables())
    courant = jnp.moveaxis(courant, 1, 0)
    me = lax.axis_index("lev").astype(jnp.int32)
    smem = pl.BlockSpec(memory_space=pltpu.SMEM)
    params = pltpu.CompilerParams(vmem_limit_bytes=40 << 20)

    def columns(n):
        return pl.BlockSpec((STEP, BINS, 256), lambda i: (i, 0, n))

    halo_shape = jax.ShapeDtypeStruct((LOCAL, BINS, 256), BF16)
    halo_spec = pl.BlockSpec((STEP, BINS, 256), lambda i: (i, 0, 0))
    wide_spec = pl.BlockSpec((STEP, BINS, 512), lambda i: (i, 0, 0))
    row_spec = pl.BlockSpec((4, STEP, BINS, NX), lambda i: (0, i, 0, 0))
    courant_spec = pl.BlockSpec((STEP, 2, 1024), lambda i: (i, 0, 0))
    table_specs = [smem, whole((2 * BINS, BINS)), whole((BINS, 2 * BINS))]
    wide, lo, hi = pl.pallas_call(
        edge_kernel,
        grid=(LOCAL // STEP,),
        out_shape=(jax.ShapeDtypeStruct((LOCAL, BINS, 512), F32), halo_shape, halo_shape),
        in_specs=table_specs + [columns(0), columns(0), columns(3), columns(3)],
        out_specs=(wide_spec, halo_spec, halo_spec),
        compiler_params=params,
        cost_estimate=pl.CostEstimate(flops=600_000_000, bytes_accessed=5_000_000, transcendentals=0),
        name="edge",
    )(coag_rate, forward, inverse, cotangent, particles, cotangent, particles)
    count = lax.axis_size("tile")
    above = lax.ppermute(hi, "tile", [(i, i + 1) for i in range(count - 1)])
    below = lax.ppermute(lo, "tile", [(i + 1, i) for i in range(count - 1)])
    ready, partial = pl.pallas_call(
        inner_kernel,
        grid=(LOCAL // STEP,),
        out_shape=(
            jax.ShapeDtypeStruct((4, LOCAL, BINS, NX), BF16),
            jax.ShapeDtypeStruct((4, LOCAL, BINS, NX), F32),
        ),
        in_specs=table_specs
        + [columns(1), columns(1), columns(2), columns(2), wide_spec, courant_spec, whole((2, 1024))],
        out_specs=(row_spec, row_spec),
        scratch_shapes=[pltpu.VMEM((BINS, 1024), F32)],
        compiler_params=params,
        cost_estimate=pl.CostEstimate(flops=600_000_000, bytes_accessed=8_000_000, transcendentals=0),
        name="inner",
    )(coag_rate, forward, inverse, cotangent, particles, cotangent, particles, wide, courant, offsets)
    block_spec = pl.BlockSpec((STEP, BINS, NX), lambda i: (i, 0, 0))
    blocks = pl.pallas_call(
        finish_kernel,
        grid=(LOCAL // STEP,),
        out_shape=(jax.ShapeDtypeStruct((LOCAL, BINS, NX), BF16),) * PEERS,
        in_specs=[smem, row_spec, row_spec, halo_spec, halo_spec, courant_spec, whole((2, 1024))],
        out_specs=(block_spec,) * PEERS,
        compiler_params=params,
        cost_estimate=pl.CostEstimate(flops=2_000_000, bytes_accessed=5_000_000, transcendentals=0),
        name="finish",
    )(me[None], ready, partial, above, below, courant, offsets)
    top = cloud_top[None, :]
    arrived = [blocks[0]] + [
        lax.ppermute(blocks[turn], "lev", [(i, i ^ turn) for i in range(PEERS)]) for turn in range(1, PEERS)
    ]
    acc = None
    for turn in (0, 4, 1, 3, 2, 5, 7, 6):
        acc = mix(jnp.bitwise_xor(me, turn)[None], mass_flux, top, arrived[turn], acc)
    return acc


def solution(mesh):
    placed = (
        P("lev", None, "tile"),
        P("lev", None, "tile"),
        P("lev"),
        P(None, "lev", "tile"),
        P(None, "tile"),
        P(None, None, ("tile", "lev")),
        P(("tile", "lev")),
    )
    return jax.shard_map(
        body, mesh=mesh, in_specs=placed, out_specs=P(None, None, ("tile", "lev")), check_vma=False
    )
```

time: 173 us -> 106 us (0.61)
  the two profiles are of different devices: /device:TPU:6 before, /device:TPU:130 now
where the time goes in v1:
time: 106 us; the launch traced here: 104 us
  Pallas kernels  67.4 us (64%)
  starting transfers between devices  23.4 us (22%)
  local copies, waits for them, and re-layouts  10.4 us (10%)
  waiting for transfers between devices  3.12 us (3%)
    pallas_call x8, Pallas kernels, mix(): pl.pallas_call(functools.partial(mix_kernel, has_acc), out_shape=jax.Shap...  49.1 us
    ppermute x7, starting transfers between devices, body(): lax.ppermute(blocks[turn], 'lev', [(i, i ^ turn) for i in range(PEERS)])  16.6 us
    unnamed x32, local copies, waits for them, and re-layouts  10.4 us
    pallas_call x1, Pallas kernels, body(): pl.pallas_call(inner_kernel, grid=(LOCAL // STEP,), out_shape=(jax.ShapeD...  7.14 us
    pallas_call x1, Pallas kernels, body(): pl.pallas_call(edge_kernel, grid=(LOCAL // STEP,), out_shape=(jax.ShapeDt...  6.63 us
    ppermute x1, starting transfers between devices, body(): below = lax.ppermute(lo, 'tile', [(i + 1, i) for i in range(count - 1)])  4.85 us
    pallas_call x1, Pallas kernels, body(): pl.pallas_call(finish_kernel, grid=(LOCAL // STEP,), out_shape=(jax.Shape...  4.59 us
    ppermute x7, waiting for transfers between devices, body(): lax.ppermute(blocks[turn], 'lev', [(i, i ^ turn) for i in range(PEERS)])  3.11 us
  transfers between devices with their start and end apart: 9, of which 1 were waited for; matrix products, arithmetic and copies ran while one was open for 0% of the time, Pallas kernels for 48%

profile of v1, /device:TPU:130, one launch (start us, length us, event | category | flops | bytes accessed | tf_op | source)
XLA Modules:
  0.0 104.5 jit_solution(13374552327406233667)
XLA Ops:
  0.0 1.5 %copy-done.1 = bf16[9,96,1024]{2,1,0:T(8,128)(2,1)S(1)} copy-done((bf16[9,96,1024]{2,1,0:T(8,128)(2,1)S(1)}, bf16[9,96,1024]{2,1,0:T(8,128)(2,1)}, u32[]{:S(2)}) %copy-start.1) | copy-done | bytes 1769496
  1.5 1.5 %copy-done.3 = bf16[9,96,1024]{2,1,0:T(8,128)(2,1)S(1)} copy-done((bf16[9,96,1024]{2,1,0:T(8,128)(2,1)S(1)}, bf16[9,96,1024]{2,1,0:T(8,128)(2,1)}, u32[]{:S(2)}) %copy-start.3) | copy-done | bytes 1769496
  5.2 6.6 %edge.1 = (f32[9,96,512]{2,1,0:T(8,128)S(1)}, bf16[9,96,256]{2,1,0:T(8,128)(2,1)}, bf16[9,96,256]{2,1,0:T(8,128)(2,1)}) custom-call(f32[9]{0:T(128)S(1)} %copy-done.14, bf16[192,96]{1,0:T(8,128)(2,1)S(1)} %copy-done.8, bf16[96,192]{1,0:T(8,128)(2,1)S(1)} %copy-done.10, bf16[9,96,1024]{2,1,0:T(8,128)(2,1)S(1)} %copy-done.1, ...), custom_call_target="tpu_custom_call" | custom-call | flops 600000000 | bytes 5000000 | tf_op jit(solution)/shard_map/edge/pallas_call | solution.py:219
  11.8 1.2 %copy-done.5 = f32[9,96,512]{2,1,0:T(8,128)} copy-done((f32[9,96,512]{2,1,0:T(8,128)}, f32[9,96,512]{2,1,0:T(8,128)S(1)}, u32[]{:S(2)}) %copy-start.5) | copy-done | bytes 1769496
  13.1 1.9 %collective-permute-start = (bf16[9,96,256]{2,1,0:T(8,128)(2,1)}, bf16[9,96,256]{2,1,0:T(8,128)(2,1)}, u32[]{:S(2)}, u32[]{:S(2)}) collective-permute-start(bf16[9,96,256]{2,1,0:T(8,128)(2,1)} %get-tuple-element.21), channel_id=1, source_target_pairs={{0,1},{1,2},{2,3},{3,4},{4,5},{5,6},{6,7},{7,8},{8,9},{9,10},{10,1... | collective-permute-start | bytes 1327112 | tf_op jit(solution)/shard_map/ppermute | solution.py:230
  15.0 4.9 %collective-permute-start.1 = (bf16[9,96,256]{2,1,0:T(8,128)(2,1)}, bf16[9,96,256]{2,1,0:T(8,128)(2,1)}, u32[]{:S(2)}, u32[]{:S(2)}) collective-permute-start(bf16[9,96,256]{2,1,0:T(8,128)(2,1)} %get-tuple-element.22), channel_id=1, source_target_pairs={{1,0},{2,1},{3,2},{4,3},{5,4},{6,5},{7,6},{8,7},{9,8},{10,9},{11,1... | collective-permute-start | bytes 1327112 | tf_op jit(solution)/shard_map/ppermute | solution.py:231
  19.9 1.5 %copy-done.6 = f32[9,96,512]{2,1,0:T(8,128)S(1)} copy-done((f32[9,96,512]{2,1,0:T(8,128)S(1)}, f32[9,96,512]{2,1,0:T(8,128)}, u32[]{:S(2)}) %copy-start.6) | copy-done | bytes 1769496
  21.4 0.9 copy-done.7
  23.8 7.1 %inner.1 = (bf16[4,9,96,128]{3,2,1,0:T(8,128)(2,1)S(1)}, f32[4,9,96,128]{3,2,1,0:T(8,128)S(1)}) custom-call(f32[9]{0:T(128)S(1)} %copy-done.15, bf16[192,96]{1,0:T(8,128)(2,1)S(1)} %copy-done.9, bf16[96,192]{1,0:T(8,128)(2,1)S(1)} %copy-done.11, bf16[9,96,1024]{2,1,0:T(8,128)(2,1)S(1)} %copy-done.2, bf16[9,96,1024]{2,1,0:T(8,128)(2,1)S(1)} %copy-done.4, ...), custom_call_target="tpu_custom_call" | custom-call | flops 600000000 | bytes 8000000 | tf_op jit(solution)/shard_map/inner/pallas_call | solution.py:232
  31.0 4.6 %finish.1 = (bf16[9,96,128]{2,1,0:T(8,128)(2,1)S(1)}, bf16[9,96,128]{2,1,0:T(8,128)(2,1)S(1)}, bf16[9,96,128]{2,1,0:T(8,128)(2,1)}, bf16[9,96,128]{2,1,0:T(8,128...) custom-call(s32[1]{0:T(128)} %bitcast.2.me.source, ...), custom_call_target="tpu_custom_call" | custom-call | flops 2000000 | bytes 5000000 | tf_op jit(solution)/shard_map/finish/pallas_call | solution.py:248
  36.3 1.6 %collective-permute-start.7 = (bf16[9,96,128]{2,1,0:T(8,128)(2,1)S(1)}, bf16[9,96,128]{2,1,0:T(8,128)(2,1)S(1)}, u32[]{:S(2)}, u32[]{:S(2)}) collective-permute-start(bf16[9,96,128]{2,1,0:T(8,128)(2,1)S(1)} %get-tuple-element.28), channel_id=1, source_target_pairs={{0,32},{32,0},{64,96},{96,64},{128,160},{160,128},{192,224},{224,1... | collective-permute-start | bytes 663560 | tf_op jit(solution)/shard_map/ppermute | solution.py:260
  37.9 2.1 %collective-permute-start.6 = (bf16[9,96,128]{2,1,0:T(8,128)(2,1)}, bf16[9,96,128]{2,1,0:T(8,128)(2,1)S(1)}, u32[]{:S(2)}, u32[]{:S(2)}) collective-permute-start(bf16[9,96,128]{2,1,0:T(8,128)(2,1)} %get-tuple-element.27), channel_id=1, source_target_pairs={{0,96},{32,64},{64,32},{96,0},{128,224},{160,192},{192,160},{224,1... | collective-permute-start | bytes 663560 | tf_op jit(solution)/shard_map/ppermute | solution.py:260
  40.6 2.1 %collective-permute-start.4 = (bf16[9,96,128]{2,1,0:T(8,128)(2,1)}, bf16[9,96,128]{2,1,0:T(8,128)(2,1)S(1)}, u32[]{:S(2)}, u32[]{:S(2)}) collective-permute-start(bf16[9,96,128]{2,1,0:T(8,128)(2,1)} %get-tuple-element.25), channel_id=1, source_target_pairs={{0,160},{32,128},{64,224},{96,192},{128,32},{160,0},{192,96},{224,... | collective-permute-start | bytes 663560 | tf_op jit(solution)/shard_map/ppermute | solution.py:260
  42.8 2.2 %collective-permute-start.3 = (bf16[9,96,128]{2,1,0:T(8,128)(2,1)}, bf16[9,96,128]{2,1,0:T(8,128)(2,1)S(1)}, u32[]{:S(2)}, u32[]{:S(2)}) collective-permute-start(bf16[9,96,128]{2,1,0:T(8,128)(2,1)} %get-tuple-element.24), channel_id=1, source_target_pairs={{0,224},{32,192},{64,160},{96,128},{128,96},{160,64},{192,32},{224... | collective-permute-start | bytes 663560 | tf_op jit(solution)/shard_map/ppermute | solution.py:260
  45.0 3.1 %collective-permute-done.7.block = bf16[9,96,128]{2,1,0:T(8,128)(2,1)S(1)} collective-permute-done((bf16[9,96,128]{2,1,0:T(8,128)(2,1)S(1)}, bf16[9,96,128]{2,1,0:T(8,128)(2,1)S(1)}, u32[]{:S(2)}, u32[]{:S(2)}) %collective-permute-start.7) | collective-permute-done | bytes 221216 | tf_op jit(solution)/shard_map/ppermute | solution.py:260
  48.1 7.3 %collective-permute-start.2 = (bf16[9,96,128]{2,1,0:T(8,128)(2,1)S(1)}, bf16[9,96,128]{2,1,0:T(8,128)(2,1)S(1)}, u32[]{:S(2)}, u32[]{:S(2)}) collective-permute-start(bf16[9,96,128]{2,1,0:T(8,128)(2,1)S(1)} %get-tuple-element.23), channel_id=1, source_target_pairs={{0,192},{32,224},{64,128},{96,160},{128,64},{160,96},{192,0},{224,... | collective-permute-start | bytes 663560 | tf_op jit(solution)/shard_map/ppermute | solution.py:260
  55.4 4.0 %mix.8.refs_0_ = f32[72,96,128]{2,1,0:T(8,128)} custom-call(s32[1]{0:T(128)} %bitcast.2.me.source, bf16[72,72,128]{2,1,0:T(8,128)(2,1)S(1)} %copy-done, s32[1,128]{1,0:T(1,128)S(1)} %bitcast.12, bf16[9,96,128]{2,1,0:T(8,128)(2,1)S(1)} %get-tuple-element.30.block), custom_call_target="tpu_custom_call" | custom-call | flops 4000000 | bytes 7000000 | tf_op jit(solution)/shard_map/mix/pallas_call | solution.py:182
  59.3 6.4 %mix.9.refs_0_ = f32[72,96,128]{2,1,0:T(8,128)} custom-call(s32[1]{0:T(128)} %bitcast.9.source, bf16[72,72,128]{2,1,0:T(8,128)(2,1)S(1)} %copy-done, s32[1,128]{1,0:T(1,128)S(1)} %bitcast.13, bf16[9,96,128]{2,1,0:T(8,128)(2,1)S(1)} %collective-permute-done.8.block, f32[72,96,128]{2,1,0:T(8,128)} %mix.8.refs_0_), custom_call_target="tpu_custom_call", output_to_operand_aliasing={{}: (4, {})} | custom-call | flops 4000000 | bytes 7000000 | tf_op jit(solution)/shard_map/mix/pallas_call | solution.py:182
  65.8 6.4 %mix.10.refs_0_ = f32[72,96,128]{2,1,0:T(8,128)} custom-call(s32[1]{0:T(128)} %bitcast.8.source, bf16[72,72,128]{2,1,0:T(8,128)(2,1)S(1)} %copy-done, s32[1,128]{1,0:T(1,128)S(1)} %bitcast.14, bf16[9,96,128]{2,1,0:T(8,128)(2,1)S(1)} %collective-permute-done.7.block, f32[72,96,128]{2,1,0:T(8,128)} %mix.9.refs_0_), custom_call_target="tpu_custom_call", output_to_operand_aliasing={{}: (4, {})} | custom-call | flops 4000000 | bytes 7000000 | tf_op jit(solution)/shard_map/mix/pallas_call | solution.py:182
  72.2 6.4 %mix.11.refs_0_ = f32[72,96,128]{2,1,0:T(8,128)} custom-call(s32[1]{0:T(128)} %bitcast.7.source, bf16[72,72,128]{2,1,0:T(8,128)(2,1)S(1)} %copy-done, s32[1,128]{1,0:T(1,128)S(1)} %bitcast.15, bf16[9,96,128]{2,1,0:T(8,128)(2,1)S(1)} %collective-permute-done.6.block, f32[72,96,128]{2,1,0:T(8,128)} %mix.10.refs_0_), custom_call_target="tpu_custom_call", output_to_operand_aliasing={{}: (4, {})} | custom-call | flops 4000000 | bytes 7000000 | tf_op jit(solution)/shard_map/mix/pallas_call | solution.py:182
  78.7 6.4 %mix.12.refs_0_ = f32[72,96,128]{2,1,0:T(8,128)} custom-call(s32[1]{0:T(128)} %bitcast.6.source, bf16[72,72,128]{2,1,0:T(8,128)(2,1)S(1)} %copy-done, s32[1,128]{1,0:T(1,128)S(1)} %bitcast.16, bf16[9,96,128]{2,1,0:T(8,128)(2,1)S(1)} %collective-permute-done.5.block, f32[72,96,128]{2,1,0:T(8,128)} %mix.11.refs_0_), custom_call_target="tpu_custom_call", output_to_operand_aliasing={{}: (4, {})} | custom-call | flops 4000000 | bytes 7000000 | tf_op jit(solution)/shard_map/mix/pallas_call | solution.py:182
  85.1 6.4 %mix.13.refs_0_ = f32[72,96,128]{2,1,0:T(8,128)} custom-call(s32[1]{0:T(128)} %bitcast.5.source, bf16[72,72,128]{2,1,0:T(8,128)(2,1)S(1)} %copy-done, s32[1,128]{1,0:T(1,128)S(1)} %bitcast.17, bf16[9,96,128]{2,1,0:T(8,128)(2,1)S(1)} %collective-permute-done.4.block, f32[72,96,128]{2,1,0:T(8,128)} %mix.12.refs_0_), custom_call_target="tpu_custom_call", output_to_operand_aliasing={{}: (4, {})} | custom-call | flops 4000000 | bytes 7000000 | tf_op jit(solution)/shard_map/mix/pallas_call | solution.py:182
  91.6 6.4 %mix.14.refs_0_ = f32[72,96,128]{2,1,0:T(8,128)} custom-call(s32[1]{0:T(128)} %bitcast.4.source, bf16[72,72,128]{2,1,0:T(8,128)(2,1)S(1)} %copy-done, s32[1,128]{1,0:T(1,128)S(1)} %bitcast.18, bf16[9,96,128]{2,1,0:T(8,128)(2,1)S(1)} %collective-permute-done.3.block, f32[72,96,128]{2,1,0:T(8,128)} %mix.13.refs_0_), custom_call_target="tpu_custom_call", output_to_operand_aliasing={{}: (4, {})} | custom-call | flops 4000000 | bytes 7000000 | tf_op jit(solution)/shard_map/mix/pallas_call | solution.py:182
  98.0 6.4 %mix.15 = f32[72,96,128]{2,1,0:T(8,128)} custom-call(s32[1]{0:T(128)} %bitcast.source, bf16[72,72,128]{2,1,0:T(8,128)(2,1)S(1)} %copy-done, s32[1,128]{1,0:T(1,128)S(1)} %bitcast.19, bf16[9,96,128]{2,1,0:T(8,128)(2,1)S(1)} %collective-permute-done.2.block, f32[72,96,128]{2,1,0:T(8,128)} %mix.14.refs_0_), custom_call_target="tpu_custom_call", output_to_operand_aliasing={{}: (4, {})} | custom-call | flops 4000000 | bytes 7000000 | tf_op jit(solution)/shard_map/mix/pallas_call | solution.py:182
  (37 shorter events, 5.3 us)
Async XLA Ops:
  0.0 1.5 %copy-start.1 = (bf16[9,96,1024]{2,1,0:T(8,128)(2,1)S(1)}, bf16[9,96,1024]{2,1,0:T(8,128)(2,1)}, u32[]{:S(2)}) copy-start(bf16[9,96,1024]{2,1,0:T(8,128)(2,1)} %grad_hi.3) | copy-start | bytes 5308420
  1.5 1.5 %copy-start.3 = (bf16[9,96,1024]{2,1,0:T(8,128)(2,1)S(1)}, bf16[9,96,1024]{2,1,0:T(8,128)(2,1)}, u32[]{:S(2)}) copy-start(bf16[9,96,1024]{2,1,0:T(8,128)(2,1)} %mass_hi.3) | copy-start | bytes 5308420
  3.0 0.8 copy-start.8
  3.8 0.8 copy-start.10
  5.2 14.6 %copy-start.2 = (bf16[9,96,1024]{2,1,0:T(8,128)(2,1)S(1)}, bf16[9,96,1024]{2,1,0:T(8,128)(2,1)}, u32[]{:S(2)}) copy-start(bf16[9,96,1024]{2,1,0:T(8,128)(2,1)} %grad_hi.3) | copy-start | bytes 5308420
  5.2 14.6 %copy-start.4 = (bf16[9,96,1024]{2,1,0:T(8,128)(2,1)S(1)}, bf16[9,96,1024]{2,1,0:T(8,128)(2,1)}, u32[]{:S(2)}) copy-start(bf16[9,96,1024]{2,1,0:T(8,128)(2,1)} %mass_hi.3) | copy-start | bytes 5308420
  5.2 14.6 %copy-start.12 = (s32[2,1024]{1,0:T(2,128)S(1)}, s32[2,1024]{1,0:T(2,128)}, u32[]{:S(2)}) copy-start(s32[2,1024]{1,0:T(2,128)} %offsets.3) | copy-start | bytes 24580
  5.2 14.7 %copy-start.15 = (f32[9]{0:T(128)S(1)}, f32[9]{0:T(128)}, u32[]{:S(2)}) copy-start(f32[9]{0:T(128)} %rate.3) | copy-start | bytes 112
  11.8 1.2 %copy-start.5 = (f32[9,96,512]{2,1,0:T(8,128)}, f32[9,96,512]{2,1,0:T(8,128)S(1)}, u32[]{:S(2)}) copy-start(f32[9,96,512]{2,1,0:T(8,128)S(1)} %get-tuple-element.18.wide) | copy-start | bytes 5308420
  13.1 18.0 %collective-permute-start = (bf16[9,96,256]{2,1,0:T(8,128)(2,1)}, bf16[9,96,256]{2,1,0:T(8,128)(2,1)}, u32[]{:S(2)}, u32[]{:S(2)}) collective-permute-start(bf16[9,96,256]{2,1,0:T(8,128)(2,1)} %get-tuple-element.21), channel_id=1, source_target_pairs={{0,1},{1,2},{2,3},{3,4},{4,5},{5,6},{6,7},{7,8},{8,9},{9,10},{10,1... | collective-permute-start | bytes 1327112 | tf_op jit(solution)/shard_map/ppermute | solution.py:230
  15.0 16.1 %collective-permute-start.1 = (bf16[9,96,256]{2,1,0:T(8,128)(2,1)}, bf16[9,96,256]{2,1,0:T(8,128)(2,1)}, u32[]{:S(2)}, u32[]{:S(2)}) collective-permute-start(bf16[9,96,256]{2,1,0:T(8,128)(2,1)} %get-tuple-element.22), channel_id=1, source_target_pairs={{1,0},{2,1},{3,2},{4,3},{5,4},{6,5},{7,6},{8,7},{9,8},{10,9},{11,1... | collective-permute-start | bytes 1327112 | tf_op jit(solution)/shard_map/ppermute | solution.py:231
  19.9 1.5 %copy-start.6 = (f32[9,96,512]{2,1,0:T(8,128)S(1)}, f32[9,96,512]{2,1,0:T(8,128)}, u32[]{:S(2)}) copy-start(f32[9,96,512]{2,1,0:T(8,128)} %copy-done.5) | copy-start | bytes 5308420
  21.4 0.9 copy-start.7
  22.2 0.8 copy-start.9
  23.0 0.8 copy-start.11
  31.0 24.4 %copy-start = (bf16[72,72,128]{2,1,0:T(8,128)(2,1)S(1)}, bf16[72,72,128]{2,1,0:T(8,128)(2,1)}, u32[]{:S(2)}) copy-start(bf16[72,72,128]{2,1,0:T(8,128)(2,1)} %flux.15) | copy-start | bytes 3981316
  31.0 24.4 %copy-start.13 = (s32[128]{0:T(128)S(1)}, s32[128]{0:T(128)}, u32[]{:S(2)}) copy-start(s32[128]{0:T(128)} %param.15) | copy-start | bytes 1540
  35.6 7.1 %collective-permute-start.8 = (bf16[9,96,128]{2,1,0:T(8,128)(2,1)S(1)}, bf16[9,96,128]{2,1,0:T(8,128)(2,1)S(1)}, u32[]{:S(2)}, u32[]{:S(2)}) collective-permute-start(bf16[9,96,128]{2,1,0:T(8,128)(2,1)S(1)} %get-tuple-element.29), channel_id=1, source_target_pairs={{0,128},{32,160},{64,192},{96,224},{128,0},{160,32},{192,64},{224,... | collective-permute-start | bytes 663560 | tf_op jit(solution)/shard_map/ppermute | solution.py:260
  36.3 11.8 %collective-permute-start.7 = (bf16[9,96,128]{2,1,0:T(8,128)(2,1)S(1)}, bf16[9,96,128]{2,1,0:T(8,128)(2,1)S(1)}, u32[]{:S(2)}, u32[]{:S(2)}) collective-permute-start(bf16[9,96,128]{2,1,0:T(8,128)(2,1)S(1)} %get-tuple-element.28), channel_id=1, source_target_pairs={{0,32},{32,0},{64,96},{96,64},{128,160},{160,128},{192,224},{224,1... | collective-permute-start | bytes 663560 | tf_op jit(solution)/shard_map/ppermute | solution.py:260
  37.9 34.4 %collective-permute-start.6 = (bf16[9,96,128]{2,1,0:T(8,128)(2,1)}, bf16[9,96,128]{2,1,0:T(8,128)(2,1)S(1)}, u32[]{:S(2)}, u32[]{:S(2)}) collective-permute-start(bf16[9,96,128]{2,1,0:T(8,128)(2,1)} %get-tuple-element.27), channel_id=1, source_target_pairs={{0,96},{32,64},{64,32},{96,0},{128,224},{160,192},{192,160},{224,1... | collective-permute-start | bytes 663560 | tf_op jit(solution)/shard_map/ppermute | solution.py:260
  39.9 38.7 %collective-permute-start.5 = (bf16[9,96,128]{2,1,0:T(8,128)(2,1)}, bf16[9,96,128]{2,1,0:T(8,128)(2,1)S(1)}, u32[]{:S(2)}, u32[]{:S(2)}) collective-permute-start(bf16[9,96,128]{2,1,0:T(8,128)(2,1)} %get-tuple-element.26), channel_id=1, source_target_pairs={{0,64},{32,96},{64,0},{96,32},{128,192},{160,224},{192,128},{224,1... | collective-permute-start | bytes 663560 | tf_op jit(solution)/shard_map/ppermute | solution.py:260
  40.6 44.5 %collective-permute-start.4 = (bf16[9,96,128]{2,1,0:T(8,128)(2,1)}, bf16[9,96,128]{2,1,0:T(8,128)(2,1)S(1)}, u32[]{:S(2)}, u32[]{:S(2)}) collective-permute-start(bf16[9,96,128]{2,1,0:T(8,128)(2,1)} %get-tuple-element.25), channel_id=1, source_target_pairs={{0,160},{32,128},{64,224},{96,192},{128,32},{160,0},{192,96},{224,... | collective-permute-start | bytes 663560 | tf_op jit(solution)/shard_map/ppermute | solution.py:260
  42.8 48.8 %collective-permute-start.3 = (bf16[9,96,128]{2,1,0:T(8,128)(2,1)}, bf16[9,96,128]{2,1,0:T(8,128)(2,1)S(1)}, u32[]{:S(2)}, u32[]{:S(2)}) collective-permute-start(bf16[9,96,128]{2,1,0:T(8,128)(2,1)} %get-tuple-element.24), channel_id=1, source_target_pairs={{0,224},{32,192},{64,160},{96,128},{128,96},{160,64},{192,32},{224... | collective-permute-start | bytes 663560 | tf_op jit(solution)/shard_map/ppermute | solution.py:260
  48.1 50.0 %collective-permute-start.2 = (bf16[9,96,128]{2,1,0:T(8,128)(2,1)S(1)}, bf16[9,96,128]{2,1,0:T(8,128)(2,1)S(1)}, u32[]{:S(2)}, u32[]{:S(2)}) collective-permute-start(bf16[9,96,128]{2,1,0:T(8,128)(2,1)S(1)} %get-tuple-element.23), channel_id=1, source_target_pairs={{0,192},{32,224},{64,128},{96,160},{128,64},{160,96},{192,0},{224,... | collective-permute-start | bytes 663560 | tf_op jit(solution)/shard_map/ppermute | solution.py:260
  (1 other events, 0.7 us)

commit v2 on v1

v2 whole, which is shorter than its diff:
```python
import functools
import math

import jax
import jax.numpy as jnp
import ml_dtypes
import numpy as np
from jax import lax
from jax.experimental import pallas as pl
from jax.experimental.pallas import tpu as pltpu
from jax.sharding import PartitionSpec as P

NX = 128
ROWS = 8
REACH = 2
BINS = 96
LOCAL = 9
LEVELS = 72
PEERS = 8
STEP = 3
HALF = 512
SUB = 6
OUTER = ((0, -2), (0, -1), (1, -2), (6, 2), (7, 1), (7, 2))
PART = 48
ORDER = (0, 4, 3, 5, 2, 6, 7, 1)
AHEAD = 8
BF16 = jnp.bfloat16
F32 = jnp.float32


def tables():
    length = 2 * BINS
    freq, bins = np.arange(BINS)[:, None], np.arange(BINS)[None, :]
    theta = 2.0 * math.pi * ((freq * bins) % length) / length
    nyquist = 1.0 - 2.0 * (np.arange(BINS) % 2)
    cos, sin = np.cos(theta), -np.sin(theta)
    sin[0] = nyquist
    forward = np.concatenate([cos, sin], axis=0)
    weight = np.where(np.arange(BINS) == 0, 1.0, 2.0)[:, None] / length
    inverse = np.concatenate([cos * weight, sin * weight], axis=0).T
    return forward.astype(ml_dtypes.bfloat16), np.ascontiguousarray(inverse).astype(ml_dtypes.bfloat16)


def adjoint_of(forward, inverse, gradient, amounts, coefficient):
    grad_spec = jnp.dot(forward, gradient, preferred_element_type=F32)
    mass_spec = jnp.dot(forward, amounts, preferred_element_type=F32)
    grad_re, grad_im = grad_spec[:BINS], grad_spec[BINS:]
    mass_re, mass_im = mass_spec[:BINS], mass_spec[BINS:]
    total_mass = mass_re[0:1]
    first = lax.broadcasted_iota(jnp.int32, (8, gradient.shape[1]), 0) == 0
    re_re, im_im = mass_re * grad_re, mass_im * grad_im
    prod_re = re_re + im_im
    prod_im = mass_re * grad_im - mass_im * grad_re
    prod_re = jnp.concatenate([jnp.where(first, re_re[:8], prod_re[:8]), prod_re[8:]], axis=0)
    prod_im = jnp.concatenate([jnp.where(first, im_im[:8], prod_im[:8]), prod_im[8:]], axis=0)
    prod = jnp.concatenate([prod_re.astype(BF16), prod_im.astype(BF16)], axis=0)
    correlation = jnp.dot(inverse, prod, preferred_element_type=F32)
    grad_wide = gradient.astype(F32)
    inner = jnp.sum(grad_wide * amounts.astype(F32), axis=0, keepdims=True)
    return grad_wide + coefficient * (correlation - grad_wide * total_mass - inner)


def group_copies(pairs, sems, group, low):
    span = pl.ds(group * STEP, STEP)
    width = HALF // len(low)
    return [
        pltpu.make_async_copy(
            source.at[span, :, start : start + width],
            target.at[span, :, side * width : (side + 1) * width],
            sems.at[group, n, side],
        )
        for n, (source, target) in enumerate(pairs)
        for side, start in enumerate(low)
    ]


def begin(copies):
    for copy in copies:
        copy.start()


def finish_copies(copies):
    for copy in copies:
        copy.wait()


def edge_kernel(rate, forward, inverse, cotangent, particles, wide, lo, hi, *scratch):
    grad, mass, forward_in, inverse_in, rate_in, sems, small_sems = scratch
    pairs = ((cotangent, grad), (particles, mass))
    small = [
        pltpu.make_async_copy(source, target, small_sems.at[n])
        for n, (source, target) in enumerate(((rate, rate_in), (forward, forward_in), (inverse, inverse_in)))
    ]
    begin(group_copies(pairs, sems, 0, (0, 768)) + small)
    finish_copies(small)

    def some(group, carry):
        finish_copies(group_copies(pairs, sems, group, (0, 768)))

        @pl.when(group < LOCAL // STEP - 1)
        def _():
            begin(group_copies(pairs, sems, group + 1, (0, 768)))

        for j in range(STEP):
            level = group * STEP + j
            adjoint = adjoint_of(forward_in[...], inverse_in[...], grad[level], mass[level], rate_in[level])
            wide[level] = adjoint
            lo[level] = adjoint[:, :256].astype(BF16)
            hi[level] = adjoint[:, 256:].astype(BF16)
        return carry

    lax.fori_loop(0, LOCAL // STEP, some, 0)


def inner_kernel(rate, forward, inverse, cotangent, particles, wide, courant, offsets, ready, partial, outer, *scratch):
    grad, mass, forward_in, inverse_in, courant_in, offsets_in, cells, sems, small_sems = scratch
    lane = lax.broadcasted_iota(jnp.int32, (1, NX), 1)
    pairs = ((cotangent, grad), (particles, mass))
    ins = ((forward, forward_in), (inverse, inverse_in), (courant, courant_in), (offsets, offsets_in))
    small = [pltpu.make_async_copy(source, target, small_sems.at[n]) for n, (source, target) in enumerate(ins)]
    begin(group_copies(pairs, sems, 0, (256,)) + small)
    finish_copies(small)
    for n, (row, upwind) in enumerate(OUTER):
        span = slice(row * NX, (row + 1) * NX)
        outer[n] = jnp.where(offsets_in[0:1, span] == upwind, courant_in[:, 0, span], 0.0)

    def near(level, j, row):
        if 2 <= row < 6:
            return cells[j, :, (row - 2) * NX : (row - 1) * NX]
        edge = row if row < 2 else row - 4
        return wide[level, :, edge * NX : (edge + 1) * NX]

    def some(group, carry):
        finish_copies(group_copies(pairs, sems, group, (256,)))

        @pl.when(group < LOCAL // STEP - 1)
        def _():
            begin(group_copies(pairs, sems, group + 1, (256,)))

        for j in range(STEP):
            level = group * STEP + j
            cells[j] = adjoint_of(forward_in[...], inverse_in[...], grad[level], mass[level], rate[level])
        for j in range(STEP):
            level = group * STEP + j
            for row in range(ROWS):
                span = slice(row * NX, (row + 1) * NX)
                cour_y, cour_x = courant_in[level, 0:1, span], courant_in[level, 1:2, span]
                shift_y, shift_x = offsets_in[0:1, span], offsets_in[1:2, span]
                centre = near(level, j, row)
                still = jnp.where(shift_y == 0, cour_y, 0.0)
                total = centre * (1.0 - cour_y - cour_x + still)
                for upwind in (-2, -1, 1, 2):
                    if 0 <= row + upwind < ROWS:
                        weight = jnp.where(shift_y == upwind, cour_y, 0.0)
                        total = total + near(level, j, row + upwind) * weight
                place = lane + shift_x
                weight = jnp.where((place >= 0) & (place < NX), cour_x, 0.0)
                place = jnp.broadcast_to(jnp.clip(place, 0, NX - 1), centre.shape)
                along_x = jnp.take_along_axis(centre, place, axis=1, mode="promise_in_bounds")
                total = total + along_x * weight
                if 2 <= row < 6:
                    ready[row - 2, level] = total.astype(BF16)
                else:
                    partial[row if row < 2 else row - 4, level] = total
        return carry

    lax.fori_loop(0, LOCAL // STEP, some, 0)


def finish_kernel(ready, partial, above, below, outer, *outs):
    me = lax.axis_index("lev")
    edges = (
        (0, ((above, 0, 0), (above, 1, 1))),
        (1, ((above, 1, 2),)),
        (6, ((below, 0, 3),)),
        (7, ((below, 0, 4), (below, 1, 5))),
    )

    def inside(row, out):
        for j in range(LOCAL):
            out[j] = ready[row - 2, j]

    def outside(edge, terms, out):
        for j in range(LOCAL):
            total = partial[edge, j]
            for ref, line, n in terms:
                total = total + ref[j, :, line * NX : (line + 1) * NX].astype(F32) * outer[n, j : j + 1]
            out[j] = total.astype(BF16)

    for turn in range(PEERS):
        row = jnp.bitwise_xor(me, turn)
        pl.when((row >= 2) & (row < 6))(functools.partial(inside, row, outs[turn]))
        for edge, (place, terms) in enumerate(edges):
            pl.when(row == place)(functools.partial(outside, edge, terms, outs[turn]))


def mix_kernel(first, last, waits, source, flux, cloud_top, block, *refs):
    refs = list(refs)
    acc = None if first else refs.pop(0)
    if waits:
        del refs[0], refs[1]
    out, weights, wide = refs[:3]
    top = cloud_top[...]
    levels = lax.broadcasted_iota(jnp.int32, (LEVELS, NX), 0)
    inside = levels <= top
    for o in range(LOCAL):
        level = source[0] * LOCAL + o
        kept = jnp.where(inside & (level <= top), flux[level].astype(F32), 0.0)
        weights[o] = kept + jnp.where(levels == level, 1.0, 0.0)
        wide[o] = block[o].astype(F32)
    held = refs[3] if last else out

    def to_out(q):
        span = pl.ds(q * SUB, SUB)
        return pltpu.make_async_copy(held.at[span], out.at[span], refs[4].at[q])

    def some(q, carry):
        row = q * SUB
        for low in range(0, BINS, PART):
            span = slice(low, low + PART)
            sums = [None if first else acc[row + n, span] for n in range(SUB)]
            for o in range(LOCAL):
                data = wide[o, span]
                for n in range(SUB):
                    term = data * weights[o, pl.ds(row + n, 1), :]
                    sums[n] = term if sums[n] is None else sums[n] + term
            for n in range(SUB):
                held[row + n, span] = sums[n]
        if last:
            to_out(q).start()
        return carry

    lax.fori_loop(0, LEVELS // SUB, some, 0)
    if last:

        def finished(q, carry):
            to_out(q).wait()
            return carry

        lax.fori_loop(0, LEVELS // SUB, finished, 0)


def near_core(x):
    return pltpu.with_memory_space_constraint(x, pltpu.VMEM)


VM = pl.BlockSpec(memory_space=pltpu.VMEM)
SM = pl.BlockSpec(memory_space=pltpu.SMEM)
FAR = pl.BlockSpec(memory_space=pltpu.HBM)


def mix(source, flux, cloud_top, block, acc, waiting, last):
    first = acc is None
    shape = (LEVELS, BINS, NX)
    scratch = [pltpu.VMEM((LOCAL, LEVELS, NX), F32), pltpu.VMEM((LOCAL, BINS, NX), F32)]
    if last:
        scratch += [pltpu.VMEM(shape, F32), pltpu.SemaphoreType.DMA((LEVELS // SUB,))]
    chained = [x for x in (acc, waiting) if x is not None]
    outs = [jax.ShapeDtypeStruct(shape, F32) if last else pltpu.VMEM(shape, F32)]
    aliases = {} if first or last else {4: 0}
    if waiting is not None:
        outs.append(pltpu.VMEM(waiting.shape, waiting.dtype))
        aliases[3 + len(chained)] = 1
    made = pl.pallas_call(
        functools.partial(mix_kernel, first, last, waiting is not None),
        out_shape=tuple(outs),
        in_specs=[SM, VM, VM, VM] + [VM] * len(chained),
        out_specs=(FAR if last else VM,) * len(outs),
        scratch_shapes=scratch,
        input_output_aliases=aliases,
        compiler_params=pltpu.CompilerParams(vmem_limit_bytes=12 << 20),
        cost_estimate=pl.CostEstimate(flops=1500000000, bytes_accessed=7000000, transcendentals=0),
        name="mix",
    )(source, near_core(flux), near_core(cloud_top), near_core(block), *chained)
    return made[0], made[-1]


def body(cotangent, particles, coag_rate, courant, offsets, mass_flux, cloud_top):
    forward, inverse = (jnp.asarray(t) for t in tables())
    courant = jnp.moveaxis(courant, 1, 0)
    me = lax.axis_index("lev").astype(jnp.int32)
    params = pltpu.CompilerParams(vmem_limit_bytes=10 << 20)
    half = pltpu.VMEM((LOCAL, BINS, HALF), BF16)
    quarter = pltpu.VMEM((LOCAL, BINS, 256), BF16)
    table_scratch = [pltpu.VMEM((2 * BINS, BINS), BF16), pltpu.VMEM((BINS, 2 * BINS), BF16)]
    groups = LOCAL // STEP
    far = functools.partial(pltpu.with_memory_space_constraint, memory_space=pltpu.HBM)
    inputs = [far(x) for x in (forward, inverse, cotangent, particles)]
    wide, lo, hi = pl.pallas_call(
        edge_kernel,
        out_shape=(pltpu.VMEM((LOCAL, BINS, HALF), F32), quarter, quarter),
        in_specs=[FAR] * 5,
        out_specs=(VM,) * 3,
        scratch_shapes=[
            half,
            half,
            *table_scratch,
            pltpu.SMEM((LOCAL,), F32),
            pltpu.SemaphoreType.DMA((groups, 2, 2)),
            pltpu.SemaphoreType.DMA((3,)),
        ],
        compiler_params=params,
        cost_estimate=pl.CostEstimate(flops=600_000_000, bytes_accessed=5_000_000, transcendentals=0),
        name="edge",
    )(far(coag_rate), *inputs)
    count = lax.axis_size("tile")
    above = lax.ppermute(hi, "tile", [(i, i + 1) for i in range(count - 1)])
    below = lax.ppermute(lo, "tile", [(i + 1, i) for i in range(count - 1)])
    ready, partial, outer = pl.pallas_call(
        inner_kernel,
        out_shape=(
            pltpu.VMEM((4, LOCAL, BINS, NX), BF16),
            pltpu.VMEM((4, LOCAL, BINS, NX), F32),
            pltpu.VMEM((len(OUTER), LOCAL, NX), F32),
        ),
        in_specs=[SM] + [FAR] * 4 + [VM] + [FAR] * 2,
        out_specs=(VM,) * 3,
        scratch_shapes=[
            half,
            half,
            *table_scratch,
            pltpu.VMEM((LOCAL, 2, 1024), F32),
            pltpu.VMEM((2, 1024), jnp.int32),
            pltpu.VMEM((STEP, BINS, HALF), F32),
            pltpu.SemaphoreType.DMA((groups, 2, 1)),
            pltpu.SemaphoreType.DMA((4,)),
        ],
        compiler_params=params,
        cost_estimate=pl.CostEstimate(flops=600_000_000, bytes_accessed=8_000_000, transcendentals=0),
        name="inner",
    )(coag_rate, *inputs, wide, far(courant), far(offsets))
    blocks = pl.pallas_call(
        finish_kernel,
        out_shape=(pltpu.VMEM((LOCAL, BINS, NX), BF16),) * PEERS,
        in_specs=[VM] * 5,
        out_specs=(VM,) * PEERS,
        compiler_params=params,
        cost_estimate=pl.CostEstimate(flops=2_000_000, bytes_accessed=5_000_000, transcendentals=0),
        name="finish",
    )(ready, partial, near_core(above), near_core(below), outer)
    top = cloud_top[None, :]
    blocks = list(blocks)
    arrived = {0: blocks[0]}

    def send(turn):
        arrived[turn] = lax.ppermute(blocks[turn], "lev", [(i, i ^ turn) for i in range(PEERS)])

    for turn in ORDER[1:AHEAD]:
        send(turn)
    acc = None
    for n, turn in enumerate(ORDER):
        later = ORDER[AHEAD + n] if AHEAD + n < PEERS else None
        waiting = None if later is None else blocks[later]
        source = jnp.bitwise_xor(me, turn)[None]
        acc, passed = mix(source, mass_flux, top, arrived[turn], acc, waiting, n == PEERS - 1)
        if later is not None:
            blocks[later] = passed
            send(later)
    return acc


def solution(mesh):
    placed = (
        P("lev", None, "tile"),
        P("lev", None, "tile"),
        P("lev"),
        P(None, "lev", "tile"),
        P(None, "tile"),
        P(None, None, ("tile", "lev")),
        P(("tile", "lev")),
    )
    return jax.shard_map(
        body, mesh=mesh, in_specs=placed, out_specs=P(None, None, ("tile", "lev")), check_vma=False
    )
```

time: 106 us -> 55.3 us (0.52)
  the two profiles are of different devices: /device:TPU:130 before, /device:TPU:6 now
where the time goes in v2:
time: 55.3 us; the launch traced here: 54.3 us
  Pallas kernels  29.9 us (54%)
  starting transfers between devices  20.8 us (38%)
  waiting for transfers between devices  3.49 us (6%)
    pallas_call x8, Pallas kernels, mix(): pl.pallas_call(functools.partial(mix_kernel, first, last, waiting is not...  19.1 us
    ppermute x7, starting transfers between devices, send(): lax.ppermute(blocks[turn], 'lev', [(i, i ^ turn) for i in range(PEERS)])  10.8 us
    ppermute x1, starting transfers between devices, body(): below = lax.ppermute(lo, 'tile', [(i + 1, i) for i in range(count - 1)])  8.05 us
    pallas_call x1, Pallas kernels, body(): pl.pallas_call(inner_kernel, out_shape=(pltpu.VMEM((4, LOCAL, BINS, NX),...  5.71 us
    pallas_call x1, Pallas kernels, body(): pl.pallas_call(edge_kernel, out_shape=(pltpu.VMEM((LOCAL, BINS, HALF), F3...  4.55 us
    ppermute x7, waiting for transfers between devices, send(): lax.ppermute(blocks[turn], 'lev', [(i, i ^ turn) for i in range(PEERS)])  3.46 us
    ppermute x1, starting transfers between devices, body(): above = lax.ppermute(hi, 'tile', [(i, i + 1) for i in range(count - 1)])  1.92 us
  transfers between devices with their start and end apart: 9, of which 1 were waited for; matrix products, arithmetic and copies ran while one was open for 0% of the time, Pallas kernels for 40%

profile of v2, /device:TPU:6, one launch (start us, length us, event | category | flops | bytes accessed | tf_op | source)
XLA Modules:
  0.0 54.3 jit_solution(818603796515798888)
XLA Ops:
  0.0 4.6 %edge.1 = (f32[9,96,512]{2,1,0:T(8,128)S(1)}, bf16[9,96,256]{2,1,0:T(8,128)(2,1)S(1)}, bf16[9,96,256]{2,1,0:T(8,128)(2,1)S(1)}) custom-call(f32[9]{0:T(128)} %rate.3, bf16[192,96]{1,0:T(8,128)(2,1)} %constant.24.clone.forward, bf16[96,192]{1,0:T(8,128)(2,1)} %constant.25.clone.inverse, bf16[9,96,1024]{2,1,0:T(8,128)(2,1)} %cotangent.3, ...), custom_call_target="tpu_custom_call" | custom-call | flops 600000000 | bytes 5000000 | tf_op jit(solution)/shard_map/edge/pallas_call | solution.py:289
  4.6 1.9 %collective-permute-start = (bf16[9,96,256]{2,1,0:T(8,128)(2,1)S(1)}, bf16[9,96,256]{2,1,0:T(8,128)(2,1)S(1)}, u32[]{:S(2)}, u32[]{:S(2)}) collective-permute-start(bf16[9,96,256]{2,1,0:T(8,128)(2,1)S(1)} %get-tuple-element.22), channel_id=1, source_target_pairs={{0,1},{1,2},{2,3},{3,4},{4,5},{5,6},{6,7},{7,8},{8,9},{9,10},{10,1... | collective-permute-start | bytes 1327112 | tf_op jit(solution)/shard_map/ppermute | solution.py:307
  6.5 8.0 %collective-permute-start.1 = (bf16[9,96,256]{2,1,0:T(8,128)(2,1)S(1)}, bf16[9,96,256]{2,1,0:T(8,128)(2,1)S(1)}, u32[]{:S(2)}, u32[]{:S(2)}) collective-permute-start(bf16[9,96,256]{2,1,0:T(8,128)(2,1)S(1)} %get-tuple-element.23), channel_id=1, source_target_pairs={{1,0},{2,1},{3,2},{4,3},{5,4},{6,5},{7,6},{8,7},{9,8},{10,9},{11,1... | collective-permute-start | bytes 1327112 | tf_op jit(solution)/shard_map/ppermute | solution.py:308
  14.6 0.0 copy-start
  14.6 0.0 copy-start.1
  14.6 5.7 %inner.1 = (bf16[4,9,96,128]{3,2,1,0:T(8,128)(2,1)S(1)}, f32[4,9,96,128]{3,2,1,0:T(8,128)S(1)}, f32[6,9,128]{2,1,0:T(8,128)S(1)}) custom-call(f32[9]{0:T(128)S(1)} %copy-done.2, bf16[192,96]{1,0:T(8,128)(2,1)} %constant.24.clone.forward, bf16[96,192]{1,0:T(8,128)(2,1)} %constant.25.clone.inverse, bf16[9,96,1024]{2,1,0:T(8,128)(2,1)} %cotangent.3, ...), custom_call_target="tpu_custom_call" | custom-call | flops 600000000 | bytes 8000000 | tf_op jit(solution)/shard_map/inner/pallas_call | solution.py:309
  20.3 0.0 collective-permute-done.1.below
  20.3 0.6 %finish.1 = (bf16[9,96,128]{2,1,0:T(8,128)(2,1)S(1)}, bf16[9,96,128]{2,1,0:T(8,128)(2,1)S(1)}, bf16[9,96,128]{2,1,0:T(8,128)(2,1)S(1)}, bf16[9,96,128]{2,1,0:T(8...) custom-call(bf16[4,9,96,128]{3,2,1,0:T(8,128)(2,1)S(1)} %get-tuple-e, ...), custom_call_target="tpu_custom_call" | custom-call | flops 2000000 | bytes 5000000 | tf_op jit(solution)/shard_map/finish/pallas_call | solution.py:332
  20.9 0.1 collective-permute-start.8
  21.0 3.1 %collective-permute-start.7 = (bf16[9,96,128]{2,1,0:T(8,128)(2,1)S(1)}, bf16[9,96,128]{2,1,0:T(8,128)(2,1)S(1)}, u32[]{:S(2)}, u32[]{:S(2)}) collective-permute-start(bf16[9,96,128]{2,1,0:T(8,128)(2,1)S(1)} %get-tuple-element.30), channel_id=1, source_target_pairs={{0,96},{32,64},{64,32},{96,0},{128,224},{160,192},{192,160},{224,1... | collective-permute-start | bytes 663560 | tf_op jit(solution)/shard_map/ppermute | solution.py:346
  24.1 1.5 %collective-permute-start.6 = (bf16[9,96,128]{2,1,0:T(8,128)(2,1)S(1)}, bf16[9,96,128]{2,1,0:T(8,128)(2,1)S(1)}, u32[]{:S(2)}, u32[]{:S(2)}) collective-permute-start(bf16[9,96,128]{2,1,0:T(8,128)(2,1)S(1)} %get-tuple-element.29), channel_id=1, source_target_pairs={{0,160},{32,128},{64,224},{96,192},{128,32},{160,0},{192,96},{224,... | collective-permute-start | bytes 663560 | tf_op jit(solution)/shard_map/ppermute | solution.py:346
  25.6 1.6 %collective-permute-start.5 = (bf16[9,96,128]{2,1,0:T(8,128)(2,1)S(1)}, bf16[9,96,128]{2,1,0:T(8,128)(2,1)S(1)}, u32[]{:S(2)}, u32[]{:S(2)}) collective-permute-start(bf16[9,96,128]{2,1,0:T(8,128)(2,1)S(1)} %get-tuple-element.28), channel_id=1, source_target_pairs={{0,64},{32,96},{64,0},{96,32},{128,192},{160,224},{192,128},{224,1... | collective-permute-start | bytes 663560 | tf_op jit(solution)/shard_map/ppermute | solution.py:346
  27.2 1.8 %collective-permute-start.4 = (bf16[9,96,128]{2,1,0:T(8,128)(2,1)S(1)}, bf16[9,96,128]{2,1,0:T(8,128)(2,1)S(1)}, u32[]{:S(2)}, u32[]{:S(2)}) collective-permute-start(bf16[9,96,128]{2,1,0:T(8,128)(2,1)S(1)} %get-tuple-element.27), channel_id=1, source_target_pairs={{0,192},{32,224},{64,128},{96,160},{128,64},{160,96},{192,0},{224,... | collective-permute-start | bytes 663560 | tf_op jit(solution)/shard_map/ppermute | solution.py:346
  29.0 2.3 %mix.8.refs_0_ = f32[72,96,128]{2,1,0:T(8,128)S(1)} custom-call(s32[1]{0:T(128)} %bitcast.9.source, bf16[72,72,128]{2,1,0:T(8,128)(2,1)S(1)} %copy-done, s32[1,128]{1,0:T(1,128)S(1)} %bitcast.10, bf16[9,96,128]{2,1,0:T(8,128)(2,1)S(1)} %get-tuple-element.32.block), custom_call_target="tpu_custom_call" | custom-call | flops 1500000000 | bytes 7000000 | tf_op jit(solution)/shard_map/mix/pallas_call | solution.py:264
  31.3 2.2 %collective-permute-start.3 = (bf16[9,96,128]{2,1,0:T(8,128)(2,1)S(1)}, bf16[9,96,128]{2,1,0:T(8,128)(2,1)S(1)}, u32[]{:S(2)}, u32[]{:S(2)}) collective-permute-start(bf16[9,96,128]{2,1,0:T(8,128)(2,1)S(1)} %get-tuple-element.26), channel_id=1, source_target_pairs={{0,224},{32,192},{64,160},{96,128},{128,96},{160,64},{192,32},{224... | collective-permute-start | bytes 663560 | tf_op jit(solution)/shard_map/ppermute | solution.py:346
  33.5 2.3 %mix.9.refs_0_ = f32[72,96,128]{2,1,0:T(8,128)S(1)} custom-call(s32[1]{0:T(128)} %bitcast.8.source, bf16[72,72,128]{2,1,0:T(8,128)(2,1)S(1)} %copy-done, s32[1,128]{1,0:T(1,128)S(1)} %bitcast.11, bf16[9,96,128]{2,1,0:T(8,128)(2,1)S(1)} %collective-permute-done.8.block, f32[72,96,128]{2,1,0:T(8,128)S(1)} %mix.8.refs_0_), custom_call_target="tpu_custom_call", output_to_operand_aliasing={{}: (4, {})} | custom-call | flops 1500000000 | bytes 7000000 | tf_op jit(solution)/shard_map/mix/pallas_call | solution.py:264
  35.8 0.5 collective-permute-start.2
  36.3 2.3 %mix.10.refs_0_ = f32[72,96,128]{2,1,0:T(8,128)S(1)} custom-call(s32[1]{0:T(128)} %bitcast.7.source, bf16[72,72,128]{2,1,0:T(8,128)(2,1)S(1)} %copy-done, s32[1,128]{1,0:T(1,128)S(1)} %bitcast.12, bf16[9,96,128]{2,1,0:T(8,128)(2,1)S(1)} %collective-permute-done.7.block, f32[72,96,128]{2,1,0:T(8,128)S(1)} %mix.9.refs_0_), custom_call_target="tpu_custom_call", output_to_operand_aliasing={{}: (4, {})} | custom-call | flops 1500000000 | bytes 7000000 | tf_op jit(solution)/shard_map/mix/pallas_call | solution.py:264
  38.6 2.3 %mix.11.refs_0_ = f32[72,96,128]{2,1,0:T(8,128)S(1)} custom-call(s32[1]{0:T(128)} %bitcast.6.source, bf16[72,72,128]{2,1,0:T(8,128)(2,1)S(1)} %copy-done, s32[1,128]{1,0:T(1,128)S(1)} %bitcast.13, bf16[9,96,128]{2,1,0:T(8,128)(2,1)S(1)} %collective-permute-done.6.block, f32[72,96,128]{2,1,0:T(8,128)S(1)} %mix.10.refs_0_), custom_call_target="tpu_custom_call", output_to_operand_aliasing={{}: (4, {})} | custom-call | flops 1500000000 | bytes 7000000 | tf_op jit(solution)/shard_map/mix/pallas_call | solution.py:264
  40.8 3.4 %collective-permute-done.5.block = bf16[9,96,128]{2,1,0:T(8,128)(2,1)S(1)} collective-permute-done((bf16[9,96,128]{2,1,0:T(8,128)(2,1)S(1)}, bf16[9,96,128]{2,1,0:T(8,128)(2,1)S(1)}, u32[]{:S(2)}, u32[]{:S(2)}) %collective-permute-start.5) | collective-permute-done | bytes 221216 | tf_op jit(solution)/shard_map/ppermute | solution.py:346
  44.3 2.3 %mix.12.refs_0_ = f32[72,96,128]{2,1,0:T(8,128)S(1)} custom-call(s32[1]{0:T(128)} %bitcast.5.source, bf16[72,72,128]{2,1,0:T(8,128)(2,1)S(1)} %copy-done, s32[1,128]{1,0:T(1,128)S(1)} %bitcast.14, bf16[9,96,128]{2,1,0:T(8,128)(2,1)S(1)} %collective-permute-done.5.block, f32[72,96,128]{2,1,0:T(8,128)S(1)} %mix.11.refs_0_), custom_call_target="tpu_custom_call", output_to_operand_aliasing={{}: (4, {})} | custom-call | flops 1500000000 | bytes 7000000 | tf_op jit(solution)/shard_map/mix/pallas_call | solution.py:264
  46.6 2.3 %mix.13.refs_0_ = f32[72,96,128]{2,1,0:T(8,128)S(1)} custom-call(s32[1]{0:T(128)} %bitcast.4.source, bf16[72,72,128]{2,1,0:T(8,128)(2,1)S(1)} %copy-done, s32[1,128]{1,0:T(1,128)S(1)} %bitcast.15, bf16[9,96,128]{2,1,0:T(8,128)(2,1)S(1)} %collective-permute-done.4.block, f32[72,96,128]{2,1,0:T(8,128)S(1)} %mix.12.refs_0_), custom_call_target="tpu_custom_call", output_to_operand_aliasing={{}: (4, {})} | custom-call | flops 1500000000 | bytes 7000000 | tf_op jit(solution)/shard_map/mix/pallas_call | solution.py:264
  48.8 2.3 %mix.14.refs_0_ = f32[72,96,128]{2,1,0:T(8,128)S(1)} custom-call(s32[1]{0:T(128)} %bitcast.3.source, bf16[72,72,128]{2,1,0:T(8,128)(2,1)S(1)} %copy-done, s32[1,128]{1,0:T(1,128)S(1)} %bitcast.16, bf16[9,96,128]{2,1,0:T(8,128)(2,1)S(1)} %collective-permute-done.3.block, f32[72,96,128]{2,1,0:T(8,128)S(1)} %mix.13.refs_0_), custom_call_target="tpu_custom_call", output_to_operand_aliasing={{}: (4, {})} | custom-call | flops 1500000000 | bytes 7000000 | tf_op jit(solution)/shard_map/mix/pallas_call | solution.py:264
  51.1 3.2 %mix.15 = f32[72,96,128]{2,1,0:T(8,128)} custom-call(s32[1]{0:T(128)} %bitcast.source, bf16[72,72,128]{2,1,0:T(8,128)(2,1)S(1)} %copy-done, s32[1,128]{1,0:T(1,128)S(1)} %bitcast.17, bf16[9,96,128]{2,1,0:T(8,128)(2,1)S(1)} %collective-permute-done.2.block, f32[72,96,128]{2,1,0:T(8,128)S(1)} %mix.14.refs_0_), custom_call_target="tpu_custom_call" | custom-call | flops 1500000000 | bytes 7000000 | tf_op jit(solution)/shard_map/mix/pallas_call | solution.py:264
  (11 shorter events, 0.0 us)
Async XLA Ops:
  0.0 14.6 %copy-start.2 = (f32[9]{0:T(128)S(1)}, f32[9]{0:T(128)}, u32[]{:S(2)}) copy-start(f32[9]{0:T(128)} %rate.3) | copy-start | bytes 112
  4.6 15.7 %collective-permute-start = (bf16[9,96,256]{2,1,0:T(8,128)(2,1)S(1)}, bf16[9,96,256]{2,1,0:T(8,128)(2,1)S(1)}, u32[]{:S(2)}, u32[]{:S(2)}) collective-permute-start(bf16[9,96,256]{2,1,0:T(8,128)(2,1)S(1)} %get-tuple-element.22), channel_id=1, source_target_pairs={{0,1},{1,2},{2,3},{3,4},{4,5},{5,6},{6,7},{7,8},{8,9},{9,10},{10,1... | collective-permute-start | bytes 1327112 | tf_op jit(solution)/shard_map/ppermute | solution.py:307
  6.5 13.9 %collective-permute-start.1 = (bf16[9,96,256]{2,1,0:T(8,128)(2,1)S(1)}, bf16[9,96,256]{2,1,0:T(8,128)(2,1)S(1)}, u32[]{:S(2)}, u32[]{:S(2)}) collective-permute-start(bf16[9,96,256]{2,1,0:T(8,128)(2,1)S(1)} %get-tuple-element.23), channel_id=1, source_target_pairs={{1,0},{2,1},{3,2},{4,3},{5,4},{6,5},{7,6},{8,7},{9,8},{10,9},{11,1... | collective-permute-start | bytes 1327112 | tf_op jit(solution)/shard_map/ppermute | solution.py:308
  14.6 14.4 %copy-start = (bf16[72,72,128]{2,1,0:T(8,128)(2,1)S(1)}, bf16[72,72,128]{2,1,0:T(8,128)(2,1)}, u32[]{:S(2)}) copy-start(bf16[72,72,128]{2,1,0:T(8,128)(2,1)} %flux.15) | copy-start | bytes 3981316
  14.6 14.4 %copy-start.1 = (s32[128]{0:T(128)S(1)}, s32[128]{0:T(128)}, u32[]{:S(2)}) copy-start(s32[128]{0:T(128)} %param.15) | copy-start | bytes 1540
  20.9 10.4 %collective-permute-start.8 = (bf16[9,96,128]{2,1,0:T(8,128)(2,1)S(1)}, bf16[9,96,128]{2,1,0:T(8,128)(2,1)S(1)}, u32[]{:S(2)}, u32[]{:S(2)}) collective-permute-start(bf16[9,96,128]{2,1,0:T(8,128)(2,1)S(1)} %get-tuple-element.31), channel_id=1, source_target_pairs={{0,128},{32,160},{64,192},{96,224},{128,0},{160,32},{192,64},{224,... | collective-permute-start | bytes 663560 | tf_op jit(solution)/shard_map/ppermute | solution.py:346
  21.0 14.7 %collective-permute-start.7 = (bf16[9,96,128]{2,1,0:T(8,128)(2,1)S(1)}, bf16[9,96,128]{2,1,0:T(8,128)(2,1)S(1)}, u32[]{:S(2)}, u32[]{:S(2)}) collective-permute-start(bf16[9,96,128]{2,1,0:T(8,128)(2,1)S(1)} %get-tuple-element.30), channel_id=1, source_target_pairs={{0,96},{32,64},{64,32},{96,0},{128,224},{160,192},{192,160},{224,1... | collective-permute-start | bytes 663560 | tf_op jit(solution)/shard_map/ppermute | solution.py:346
  24.1 14.5 %collective-permute-start.6 = (bf16[9,96,128]{2,1,0:T(8,128)(2,1)S(1)}, bf16[9,96,128]{2,1,0:T(8,128)(2,1)S(1)}, u32[]{:S(2)}, u32[]{:S(2)}) collective-permute-start(bf16[9,96,128]{2,1,0:T(8,128)(2,1)S(1)} %get-tuple-element.29), channel_id=1, source_target_pairs={{0,160},{32,128},{64,224},{96,192},{128,32},{160,0},{192,96},{224,... | collective-permute-start | bytes 663560 | tf_op jit(solution)/shard_map/ppermute | solution.py:346
  25.6 18.7 %collective-permute-start.5 = (bf16[9,96,128]{2,1,0:T(8,128)(2,1)S(1)}, bf16[9,96,128]{2,1,0:T(8,128)(2,1)S(1)}, u32[]{:S(2)}, u32[]{:S(2)}) collective-permute-start(bf16[9,96,128]{2,1,0:T(8,128)(2,1)S(1)} %get-tuple-element.28), channel_id=1, source_target_pairs={{0,64},{32,96},{64,0},{96,32},{128,192},{160,224},{192,128},{224,1... | collective-permute-start | bytes 663560 | tf_op jit(solution)/shard_map/ppermute | solution.py:346
  27.2 19.4 %collective-permute-start.4 = (bf16[9,96,128]{2,1,0:T(8,128)(2,1)S(1)}, bf16[9,96,128]{2,1,0:T(8,128)(2,1)S(1)}, u32[]{:S(2)}, u32[]{:S(2)}) collective-permute-start(bf16[9,96,128]{2,1,0:T(8,128)(2,1)S(1)} %get-tuple-element.27), channel_id=1, source_target_pairs={{0,192},{32,224},{64,128},{96,160},{128,64},{160,96},{192,0},{224,... | collective-permute-start | bytes 663560 | tf_op jit(solution)/shard_map/ppermute | solution.py:346
  31.3 17.5 %collective-permute-start.3 = (bf16[9,96,128]{2,1,0:T(8,128)(2,1)S(1)}, bf16[9,96,128]{2,1,0:T(8,128)(2,1)S(1)}, u32[]{:S(2)}, u32[]{:S(2)}) collective-permute-start(bf16[9,96,128]{2,1,0:T(8,128)(2,1)S(1)} %get-tuple-element.26), channel_id=1, source_target_pairs={{0,224},{32,192},{64,160},{96,128},{128,96},{160,64},{192,32},{224... | collective-permute-start | bytes 663560 | tf_op jit(solution)/shard_map/ppermute | solution.py:346
  35.8 15.3 %collective-permute-start.2 = (bf16[9,96,128]{2,1,0:T(8,128)(2,1)S(1)}, bf16[9,96,128]{2,1,0:T(8,128)(2,1)S(1)}, u32[]{:S(2)}, u32[]{:S(2)}) collective-permute-start(bf16[9,96,128]{2,1,0:T(8,128)(2,1)S(1)} %get-tuple-element.25), channel_id=1, source_target_pairs={{0,32},{32,0},{64,96},{96,64},{128,160},{160,128},{192,224},{224,1... | collective-permute-start | bytes 663560 | tf_op jit(solution)/shard_map/ppermute | solution.py:346

commit v3 on v2

--- a/solution.py
+++ b/solution.py
@@ -22,8 +22,8 @@
 SUB = 6
 OUTER = ((0, -2), (0, -1), (1, -2), (6, 2), (7, 1), (7, 2))
 PART = 48
-ORDER = (0, 4, 3, 5, 2, 6, 7, 1)
-AHEAD = 8
+SENDS = (4, 3, 5, 2, 6, 7, 1)
+ORDER = (0, 4, 3, 5, 6, 7, 1, 2)
 BF16 = jnp.bfloat16
 F32 = jnp.float32
 
@@ -84,14 +84,27 @@
         copy.wait()
 
 
-def edge_kernel(rate, forward, inverse, cotangent, particles, wide, lo, hi, *scratch):
-    grad, mass, forward_in, inverse_in, rate_in, sems, small_sems = scratch
+def edge_kernel(rate, forward, inverse, cotangent, particles, courant, offsets, *refs):
+    wide, far_rows, near_rows, grad_mid, mass_mid, forward_in, inverse_in, courant_in, offsets_in = refs[:9]
+    grad, mass, rate_in, sems, small_sems, mid_sems = refs[9:]
+    even = lax.rem(lax.axis_index("tile"), 2) == 0
     pairs = ((cotangent, grad), (particles, mass))
     small = [
         pltpu.make_async_copy(source, target, small_sems.at[n])
         for n, (source, target) in enumerate(((rate, rate_in), (forward, forward_in), (inverse, inverse_in)))
     ]
-    begin(group_copies(pairs, sems, 0, (0, 768)) + small)
+    middle = [
+        pltpu.make_async_copy(source, target, mid_sems.at[n])
+        for n, (source, target) in enumerate(
+            (
+                (cotangent.at[:, :, 256:768], grad_mid),
+                (particles.at[:, :, 256:768], mass_mid),
+                (courant, courant_in),
+                (offsets, offsets_in),
+            )
+        )
+    ]
+    begin(small + group_copies(pairs, sems, 0, (0, 768)))
     finish_copies(small)
 
     def some(group, carry):
@@ -100,29 +113,29 @@
         @pl.when(group < LOCAL // STEP - 1)
         def _():
             begin(group_copies(pairs, sems, group + 1, (0, 768)))
+
+        @pl.when(group == LOCAL // STEP - 2)
+        def _():
+            begin(middle)
 
         for j in range(STEP):
             level = group * STEP + j
             adjoint = adjoint_of(forward_in[...], inverse_in[...], grad[level], mass[level], rate_in[level])
             wide[level] = adjoint
-            lo[level] = adjoint[:, :256].astype(BF16)
-            hi[level] = adjoint[:, 256:].astype(BF16)
+            lo, hi = adjoint[:, :256], adjoint[:, 256:]
+            far_rows[level] = jnp.where(even, lo, hi).astype(BF16)
+            near_rows[level] = jnp.where(even, hi, lo).astype(BF16)
         return carry
 
     lax.fori_loop(0, LOCAL // STEP, some, 0)
-
-
-def inner_kernel(rate, forward, inverse, cotangent, particles, wide, courant, offsets, ready, partial, outer, *scratch):
-    grad, mass, forward_in, inverse_in, courant_in, offsets_in, cells, sems, small_sems = scratch
+    finish_copies(middle)
+
+
+def inner_kernel(rate, forward, inverse, cotangent, particles, wide, courant, offsets, ready, partial, outer, cells):
     lane = lax.broadcasted_iota(jnp.int32, (1, NX), 1)
-    pairs = ((cotangent, grad), (particles, mass))
-    ins = ((forward, forward_in), (inverse, inverse_in), (courant, courant_in), (offsets, offsets_in))
-    small = [pltpu.make_async_copy(source, target, small_sems.at[n]) for n, (source, target) in enumerate(ins)]
-    begin(group_copies(pairs, sems, 0, (256,)) + small)
-    finish_copies(small)
     for n, (row, upwind) in enumerate(OUTER):
         span = slice(row * NX, (row + 1) * NX)
-        outer[n] = jnp.where(offsets_in[0:1, span] == upwind, courant_in[:, 0, span], 0.0)
+        outer[n] = jnp.where(offsets[0:1, span] == upwind, courant[:, 0, span], 0.0)
 
     def near(level, j, row):
         if 2 <= row < 6:
@@ -131,21 +144,15 @@
         return wide[level, :, edge * NX : (edge + 1) * NX]
 
     def some(group, carry):
-        finish_copies(group_copies(pairs, sems, group, (256,)))
-
-        @pl.when(group < LOCAL // STEP - 1)
-        def _():
-            begin(group_copies(pairs, sems, group + 1, (256,)))
-
         for j in range(STEP):
             level = group * STEP + j
-            cells[j] = adjoint_of(forward_in[...], inverse_in[...], grad[level], mass[level], rate[level])
+            cells[j] = adjoint_of(forward[...], inverse[...], cotangent[level], particles[level], rate[level])
         for j in range(STEP):
             level = group * STEP + j
             for row in range(ROWS):
                 span = slice(row * NX, (row + 1) * NX)
-                cour_y, cour_x = courant_in[level, 0:1, span], courant_in[level, 1:2, span]
-                shift_y, shift_x = offsets_in[0:1, span], offsets_in[1:2, span]
+                cour_y, cour_x = courant[level, 0:1, span], courant[level, 1:2, span]
+                shift_y, shift_x = offsets[0:1, span], offsets[1:2, span]
                 centre = near(level, j, row)
                 still = jnp.where(shift_y == 0, cour_y, 0.0)
                 total = centre * (1.0 - cour_y - cour_x + still)
@@ -167,13 +174,19 @@
     lax.fori_loop(0, LOCAL // STEP, some, 0)
 
 
-def finish_kernel(ready, partial, above, below, outer, *outs):
+def finish_kernel(ready, partial, far_rows, near_rows, outer, *outs):
     me = lax.axis_index("lev")
+    even = lax.rem(lax.axis_index("tile"), 2) == 0
+
+    def beside(upward, j, line):
+        span = slice(line * NX, (line + 1) * NX)
+        return jnp.where(even == upward, far_rows[j, :, span], near_rows[j, :, span]).astype(F32)
+
     edges = (
-        (0, ((above, 0, 0), (above, 1, 1))),
-        (1, ((above, 1, 2),)),
-        (6, ((below, 0, 3),)),
-        (7, ((below, 0, 4), (below, 1, 5))),
+        (0, ((True, 0, 0), (True, 1, 1))),
+        (1, ((True, 1, 2),)),
+        (6, ((False, 0, 3),)),
+        (7, ((False, 0, 4), (False, 1, 5))),
     )
 
     def inside(row, out):
@@ -183,8 +196,8 @@
     def outside(edge, terms, out):
         for j in range(LOCAL):
             total = partial[edge, j]
-            for ref, line, n in terms:
-                total = total + ref[j, :, line * NX : (line + 1) * NX].astype(F32) * outer[n, j : j + 1]
+            for upward, line, n in terms:
+                total = total + beside(upward, j, line) * outer[n, j : j + 1]
             out[j] = total.astype(BF16)
 
     for turn in range(PEERS):
@@ -194,11 +207,9 @@
             pl.when(row == place)(functools.partial(outside, edge, terms, outs[turn]))
 
 
-def mix_kernel(first, last, waits, source, flux, cloud_top, block, *refs):
+def mix_kernel(first, last, source, flux, cloud_top, block, *refs):
     refs = list(refs)
     acc = None if first else refs.pop(0)
-    if waits:
-        del refs[0], refs[1]
     out, weights, wide = refs[:3]
     top = cloud_top[...]
     levels = lax.broadcasted_iota(jnp.int32, (LEVELS, NX), 0)
@@ -249,30 +260,27 @@
 FAR = pl.BlockSpec(memory_space=pltpu.HBM)
 
 
-def mix(source, flux, cloud_top, block, acc, waiting, last):
+def mix(source, flux, cloud_top, block, acc, last):
     first = acc is None
     shape = (LEVELS, BINS, NX)
     scratch = [pltpu.VMEM((LOCAL, LEVELS, NX), F32), pltpu.VMEM((LOCAL, BINS, NX), F32)]
     if last:
         scratch += [pltpu.VMEM(shape, F32), pltpu.SemaphoreType.DMA((LEVELS // SUB,))]
-    chained = [x for x in (acc, waiting) if x is not None]
-    outs = [jax.ShapeDtypeStruct(shape, F32) if last else pltpu.VMEM(shape, F32)]
-    aliases = {} if first or last else {4: 0}
-    if waiting is not None:
-        outs.append(pltpu.VMEM(waiting.shape, waiting.dtype))
-        aliases[3 + len(chained)] = 1
-    made = pl.pallas_call(
-        functools.partial(mix_kernel, first, last, waiting is not None),
-        out_shape=tuple(outs),
-        in_specs=[SM, VM, VM, VM] + [VM] * len(chained),
-        out_specs=(FAR if last else VM,) * len(outs),
+    return pl.pallas_call(
+        functools.partial(mix_kernel, first, last),
+        out_shape=jax.ShapeDtypeStruct(shape, F32) if last else pltpu.VMEM(shape, F32),
+        in_specs=[SM, VM, VM, VM] + ([] if first else [VM]),
+        out_specs=FAR if last else VM,
         scratch_shapes=scratch,
-        input_output_aliases=aliases,
+        input_output_aliases={} if first or last else {4: 0},
         compiler_params=pltpu.CompilerParams(vmem_limit_bytes=12 << 20),
-        cost_estimate=pl.CostEstimate(flops=1500000000, bytes_accessed=7000000, transcendentals=0),
+        cost_estimate=pl.CostEstimate(flops=1_500_000_000, bytes_accessed=7_000_000, transcendentals=0),
         name="mix",
-    )(source, near_core(flux), near_core(cloud_top), near_core(block), *chained)
-    return made[0], made[-1]
+    )(source, near_core(flux), near_core(cloud_top), near_core(block), *([] if first else [acc]))
+
+
+def swaps(first, count):
+    return [pair for i in range(first, count - 1, 2) for pair in ((i, i + 1), (i + 1, i))]
 
 
 def body(cotangent, particles, coag_rate, courant, offsets, mass_flux, cloud_top):
@@ -282,30 +290,34 @@
     params = pltpu.CompilerParams(vmem_limit_bytes=10 << 20)
     half = pltpu.VMEM((LOCAL, BINS, HALF), BF16)
     quarter = pltpu.VMEM((LOCAL, BINS, 256), BF16)
-    table_scratch = [pltpu.VMEM((2 * BINS, BINS), BF16), pltpu.VMEM((BINS, 2 * BINS), BF16)]
-    groups = LOCAL // STEP
+    handed = (
+        pltpu.VMEM((2 * BINS, BINS), BF16),
+        pltpu.VMEM((BINS, 2 * BINS), BF16),
+        pltpu.VMEM((LOCAL, 2, ROWS * NX), F32),
+        pltpu.VMEM((2, ROWS * NX), jnp.int32),
+    )
     far = functools.partial(pltpu.with_memory_space_constraint, memory_space=pltpu.HBM)
-    inputs = [far(x) for x in (forward, inverse, cotangent, particles)]
-    wide, lo, hi = pl.pallas_call(
+    inputs = [far(x) for x in (coag_rate, forward, inverse, cotangent, particles, courant, offsets)]
+    wide, far_rows, near_rows, grad_mid, mass_mid, forward, inverse, courant, offsets = pl.pallas_call(
         edge_kernel,
-        out_shape=(pltpu.VMEM((LOCAL, BINS, HALF), F32), quarter, quarter),
-        in_specs=[FAR] * 5,
-        out_specs=(VM,) * 3,
+        out_shape=(pltpu.VMEM((LOCAL, BINS, HALF), F32), quarter, quarter, half, half, *handed),
+        in_specs=[FAR] * 7,
+        out_specs=(VM,) * 9,
         scratch_shapes=[
             half,
             half,
-            *table_scratch,
             pltpu.SMEM((LOCAL,), F32),
-            pltpu.SemaphoreType.DMA((groups, 2, 2)),
+            pltpu.SemaphoreType.DMA((LOCAL // STEP, 2, 2)),
             pltpu.SemaphoreType.DMA((3,)),
+            pltpu.SemaphoreType.DMA((4,)),
         ],
         compiler_params=params,
         cost_estimate=pl.CostEstimate(flops=600_000_000, bytes_accessed=5_000_000, transcendentals=0),
         name="edge",
-    )(far(coag_rate), *inputs)
+    )(*inputs)
     count = lax.axis_size("tile")
-    above = lax.ppermute(hi, "tile", [(i, i + 1) for i in range(count - 1)])
-    below = lax.ppermute(lo, "tile", [(i + 1, i) for i in range(count - 1)])
+    far_rows = lax.ppermute(far_rows, "tile", swaps(1, count))
+    near_rows = lax.ppermute(near_rows, "tile", swaps(0, count))
     ready, partial, outer = pl.pallas_call(
         inner_kernel,
         out_shape=(
@@ -313,22 +325,13 @@
             pltpu.VMEM((4, LOCAL, BINS, NX), F32),
             pltpu.VMEM((len(OUTER), LOCAL, NX), F32),
         ),
-        in_specs=[SM] + [FAR] * 4 + [VM] + [FAR] * 2,
+        in_specs=[SM] + [VM] * 7,
         out_specs=(VM,) * 3,
-        scratch_shapes=[
-            half,
-            half,
-            *table_scratch,
-            pltpu.VMEM((LOCAL, 2, 1024), F32),
-            pltpu.VMEM((2, 1024), jnp.int32),
-            pltpu.VMEM((STEP, BINS, HALF), F32),
-            pltpu.SemaphoreType.DMA((groups, 2, 1)),
-            pltpu.SemaphoreType.DMA((4,)),
-        ],
+        scratch_shapes=[pltpu.VMEM((STEP, BINS, HALF), F32)],
         compiler_params=params,
         cost_estimate=pl.CostEstimate(flops=600_000_000, bytes_accessed=8_000_000, transcendentals=0),
         name="inner",
-    )(coag_rate, *inputs, wide, far(courant), far(offsets))
+    )(coag_rate, forward, inverse, grad_mid, mass_mid, wide, courant, offsets)
     blocks = pl.pallas_call(
         finish_kernel,
         out_shape=(pltpu.VMEM((LOCAL, BINS, NX), BF16),) * PEERS,
@@ -337,25 +340,15 @@
         compiler_params=params,
         cost_estimate=pl.CostEstimate(flops=2_000_000, bytes_accessed=5_000_000, transcendentals=0),
         name="finish",
-    )(ready, partial, near_core(above), near_core(below), outer)
+    )(ready, partial, near_core(far_rows), near_core(near_rows), outer)
     top = cloud_top[None, :]
-    blocks = list(blocks)
     arrived = {0: blocks[0]}
-
-    def send(turn):
+    for turn in SENDS:
         arrived[turn] = lax.ppermute(blocks[turn], "lev", [(i, i ^ turn) for i in range(PEERS)])
-
-    for turn in ORDER[1:AHEAD]:
-        send(turn)
     acc = None
-    for n, turn in enumerate(ORDER):
-        later = ORDER[AHEAD + n] if AHEAD + n < PEERS else None
-        waiting = None if later is None else blocks[later]
+    for turn in ORDER:
         source = jnp.bitwise_xor(me, turn)[None]
-        acc, passed = mix(source, mass_flux, top, arrived[turn], acc, waiting, n == PEERS - 1)
-        if later is not None:
-            blocks[later] = passed
-            send(later)
+        acc = mix(source, mass_flux, top, arrived[turn], acc, turn == ORDER[-1])
     return acc
 
 

time: 55.3 us -> 51.1 us (0.924); the launches traced: 54.3 us -> 50.8 us
  waiting for transfers between devices: 3.49 us -> 1.68 us
  Pallas kernels: 29.9 us -> 28.8 us
  starting transfers between devices: 20.8 us -> 20.1 us
    ppermute x9, waiting for transfers between devices: 3.49 us -> 1.68 us  [the longest x1 1.45 us: body(): far_rows = lax.ppermute(far_rows, 'tile', swaps(1, count))]
    pallas_call x1, Pallas kernels: 5.71 us -> 4.49 us  [body(): pl.pallas_call(inner_kernel, out_shape=(pltpu.VMEM((4, LOCAL, BINS, NX),...]
    ppermute x9, starting transfers between devices: 20.8 us -> 20.1 us  [the longest x7 12 us: body(): lax.ppermute(blocks[turn], 'lev', [(i, i ^ turn) for i in range(PEERS)])]
  transfers between devices with their start and end apart: 9 -> 9, of which waited for: 1 -> 3; matrix products, arithmetic and copies ran while one was open for 0% -> 0% of each run, Pallas kernels for 40% -> 40%
where the time goes in v3:
time: 51.1 us; the launch traced here: 50.8 us
  Pallas kernels  28.8 us (56%)
  starting transfers between devices  20.1 us (39%)
  waiting for transfers between devices  1.68 us (3%)
    pallas_call x8, Pallas kernels, mix(): pl.pallas_call(functools.partial(mix_kernel, first, last), out_shape=jax....  19.1 us
    ppermute x7, starting transfers between devices, body(): lax.ppermute(blocks[turn], 'lev', [(i, i ^ turn) for i in range(PEERS)])  12 us
    ppermute x1, starting transfers between devices, body(): far_rows = lax.ppermute(far_rows, 'tile', swaps(1, count))  8.05 us
    pallas_call x1, Pallas kernels, body(): pl.pallas_call(edge_kernel, out_shape=(pltpu.VMEM((LOCAL, BINS, HALF), F3...  4.63 us
    pallas_call x1, Pallas kernels, body(): pl.pallas_call(inner_kernel, out_shape=(pltpu.VMEM((4, LOCAL, BINS, NX),...  4.49 us
    ppermute x1, waiting for transfers between devices, body(): far_rows = lax.ppermute(far_rows, 'tile', swaps(1, count))  1.45 us
  transfers between devices with their start and end apart: 9, of which 3 were waited for; matrix products, arithmetic and copies ran while one was open for 0% of the time, Pallas kernels for 40%

profile of v3, /device:TPU:6, one launch (start us, length us, event | category | flops | bytes accessed | tf_op | source)
XLA Modules:
  0.0 50.8 jit_solution(812052949632705076)
XLA Ops:
  0.0 4.6 %edge.1 = (f32[9,96,512]{2,1,0:T(8,128)S(1)}, bf16[9,96,256]{2,1,0:T(8,128)(2,1)S(1)}, bf16[9,96,256]{2,1,0:T(8,128)(2,1)S(1)}, bf16[9,96,512]{2,1,0:T(8,128)(2,...) custom-call(f32[9]{0:T(128)} %rate.3, ...), custom_call_target="tpu_custom_call" | custom-call | flops 600000000 | bytes 5000000 | tf_op jit(solution)/shard_map/edge/pallas_call | solution.py:301
  4.6 8.0 %collective-permute-start = (bf16[9,96,256]{2,1,0:T(8,128)(2,1)S(1)}, bf16[9,96,256]{2,1,0:T(8,128)(2,1)S(1)}, u32[]{:S(2)}, u32[]{:S(2)}) collective-permute-start(bf16[9,96,256]{2,1,0:T(8,128)(2,1)S(1)} %get-tuple-element.34), channel_id=1, source_target_pairs={{1,2},{2,1},{3,4},{4,3},{5,6},{6,5},{7,8},{8,7},{9,10},{10,9},{11,... | collective-permute-start | bytes 1327112 | tf_op jit(solution)/shard_map/ppermute | solution.py:319
  12.7 0.1 collective-permute-start.1
  12.8 0.0 copy-start
  12.8 4.5 %inner.1 = (bf16[4,9,96,128]{3,2,1,0:T(8,128)(2,1)S(1)}, f32[4,9,96,128]{3,2,1,0:T(8,128)S(1)}, f32[6,9,128]{2,1,0:T(8,128)S(1)}) custom-call(f32[9]{0:T(128)S(1)} %copy-done.2, bf16[192,96]{1,0:T(8,128)(2,1)S(1)} %get-tuple-element.25.forward, bf16[96,192]{1,0:T(8,128)(2,1)S(1)} %get-tuple-element.26.inverse, ...), custom_call_target="tpu_custom_call" | custom-call | flops 600000000 | bytes 8000000 | tf_op jit(solution)/shard_map/inner/pallas_call | solution.py:321
  17.3 1.5 %collective-permute-done.far_rows = bf16[9,96,256]{2,1,0:T(8,128)(2,1)S(1)} collective-permute-done((bf16[9,96,256]{2,1,0:T(8,128)(2,1)S(1)}, bf16[9,96,256]{2,1,0:T(8,128)(2,1)S(1)}, u32[]{:S(2)}, u32[]{:S(2)}) %collective-permute-start) | collective-permute-done | bytes 442400 | tf_op jit(solution)/shard_map/ppermute | solution.py:319
  18.8 0.6 %finish.1 = (bf16[9,96,128]{2,1,0:T(8,128)(2,1)S(1)}, bf16[9,96,128]{2,1,0:T(8,128)(2,1)S(1)}, bf16[9,96,128]{2,1,0:T(8,128)(2,1)S(1)}, bf16[9,96,128]{2,1,0:T(8...) custom-call(bf16[4,9,96,128]{3,2,1,0:T(8,128)(2,1)S(1)} %get-tuple-e, ...), custom_call_target="tpu_custom_call" | custom-call | flops 2000000 | bytes 5000000 | tf_op jit(solution)/shard_map/finish/pallas_call | solution.py:335
  19.4 0.1 collective-permute-start.8
  19.5 3.1 %collective-permute-start.7 = (bf16[9,96,128]{2,1,0:T(8,128)(2,1)S(1)}, bf16[9,96,128]{2,1,0:T(8,128)(2,1)S(1)}, u32[]{:S(2)}, u32[]{:S(2)}) collective-permute-start(bf16[9,96,128]{2,1,0:T(8,128)(2,1)S(1)} %get-tuple-element.42), channel_id=1, source_target_pairs={{0,96},{32,64},{64,32},{96,0},{128,224},{160,192},{192,160},{224,1... | collective-permute-start | bytes 663560 | tf_op jit(solution)/shard_map/ppermute | solution.py:347
  22.6 1.5 %collective-permute-start.6 = (bf16[9,96,128]{2,1,0:T(8,128)(2,1)S(1)}, bf16[9,96,128]{2,1,0:T(8,128)(2,1)S(1)}, u32[]{:S(2)}, u32[]{:S(2)}) collective-permute-start(bf16[9,96,128]{2,1,0:T(8,128)(2,1)S(1)} %get-tuple-element.41), channel_id=1, source_target_pairs={{0,160},{32,128},{64,224},{96,192},{128,32},{160,0},{192,96},{224,... | collective-permute-start | bytes 663560 | tf_op jit(solution)/shard_map/ppermute | solution.py:347
  24.1 1.1 %collective-permute-start.5 = (bf16[9,96,128]{2,1,0:T(8,128)(2,1)S(1)}, bf16[9,96,128]{2,1,0:T(8,128)(2,1)S(1)}, u32[]{:S(2)}, u32[]{:S(2)}) collective-permute-start(bf16[9,96,128]{2,1,0:T(8,128)(2,1)S(1)} %get-tuple-element.40), channel_id=1, source_target_pairs={{0,192},{32,224},{64,128},{96,160},{128,64},{160,96},{192,0},{224,... | collective-permute-start | bytes 663560 | tf_op jit(solution)/shard_map/ppermute | solution.py:347
  25.2 4.4 %collective-permute-start.4 = (bf16[9,96,128]{2,1,0:T(8,128)(2,1)S(1)}, bf16[9,96,128]{2,1,0:T(8,128)(2,1)S(1)}, u32[]{:S(2)}, u32[]{:S(2)}) collective-permute-start(bf16[9,96,128]{2,1,0:T(8,128)(2,1)S(1)} %get-tuple-element.39), channel_id=1, source_target_pairs={{0,224},{32,192},{64,160},{96,128},{128,96},{160,64},{192,32},{224... | collective-permute-start | bytes 663560 | tf_op jit(solution)/shard_map/ppermute | solution.py:347
  29.6 2.3 %mix.8.refs_0_ = f32[72,96,128]{2,1,0:T(8,128)S(1)} custom-call(s32[1]{0:T(128)} %bitcast.9.source, bf16[72,72,128]{2,1,0:T(8,128)(2,1)S(1)} %copy-done, s32[1,128]{1,0:T(1,128)S(1)} %bitcast.10, bf16[9,96,128]{2,1,0:T(8,128)(2,1)S(1)} %get-tuple-element.44.block), custom_call_target="tpu_custom_call" | custom-call | flops 1500000000 | bytes 7000000 | tf_op jit(solution)/shard_map/mix/pallas_call | solution.py:269
  31.9 0.1 collective-permute-start.3
  32.0 2.3 %mix.9.refs_0_ = f32[72,96,128]{2,1,0:T(8,128)S(1)} custom-call(s32[1]{0:T(128)} %bitcast.8.source, bf16[72,72,128]{2,1,0:T(8,128)(2,1)S(1)} %copy-done, s32[1,128]{1,0:T(1,128)S(1)} %bitcast.11, bf16[9,96,128]{2,1,0:T(8,128)(2,1)S(1)} %collective-permute-done.8.block, f32[72,96,128]{2,1,0:T(8,128)S(1)} %mix.8.refs_0_), custom_call_target="tpu_custom_call", output_to_operand_aliasing={{}: (4, {})} | custom-call | flops 1500000000 | bytes 7000000 | tf_op jit(solution)/shard_map/mix/pallas_call | solution.py:269
  34.2 1.8 %collective-permute-start.2 = (bf16[9,96,128]{2,1,0:T(8,128)(2,1)S(1)}, bf16[9,96,128]{2,1,0:T(8,128)(2,1)S(1)}, u32[]{:S(2)}, u32[]{:S(2)}) collective-permute-start(bf16[9,96,128]{2,1,0:T(8,128)(2,1)S(1)} %get-tuple-element.37), channel_id=1, source_target_pairs={{0,64},{32,96},{64,0},{96,32},{128,192},{160,224},{192,128},{224,1... | collective-permute-start | bytes 663560 | tf_op jit(solution)/shard_map/ppermute | solution.py:347
  36.0 2.3 %mix.10.refs_0_ = f32[72,96,128]{2,1,0:T(8,128)S(1)} custom-call(s32[1]{0:T(128)} %bitcast.7.source, bf16[72,72,128]{2,1,0:T(8,128)(2,1)S(1)} %copy-done, s32[1,128]{1,0:T(1,128)S(1)} %bitcast.12, bf16[9,96,128]{2,1,0:T(8,128)(2,1)S(1)} %collective-permute-done.7.block, f32[72,96,128]{2,1,0:T(8,128)S(1)} %mix.9.refs_0_), custom_call_target="tpu_custom_call", output_to_operand_aliasing={{}: (4, {})} | custom-call | flops 1500000000 | bytes 7000000 | tf_op jit(solution)/shard_map/mix/pallas_call | solution.py:269
  38.3 2.3 %mix.11.refs_0_ = f32[72,96,128]{2,1,0:T(8,128)S(1)} custom-call(s32[1]{0:T(128)} %bitcast.6.source, bf16[72,72,128]{2,1,0:T(8,128)(2,1)S(1)} %copy-done, s32[1,128]{1,0:T(1,128)S(1)} %bitcast.13, bf16[9,96,128]{2,1,0:T(8,128)(2,1)S(1)} %collective-permute-done.6.block, f32[72,96,128]{2,1,0:T(8,128)S(1)} %mix.10.refs_0_), custom_call_target="tpu_custom_call", output_to_operand_aliasing={{}: (4, {})} | custom-call | flops 1500000000 | bytes 7000000 | tf_op jit(solution)/shard_map/mix/pallas_call | solution.py:269
  40.6 2.3 %mix.12.refs_0_ = f32[72,96,128]{2,1,0:T(8,128)S(1)} custom-call(s32[1]{0:T(128)} %bitcast.5.source, bf16[72,72,128]{2,1,0:T(8,128)(2,1)S(1)} %copy-done, s32[1,128]{1,0:T(1,128)S(1)} %bitcast.14, bf16[9,96,128]{2,1,0:T(8,128)(2,1)S(1)} %collective-permute-done.5.block, f32[72,96,128]{2,1,0:T(8,128)S(1)} %mix.11.refs_0_), custom_call_target="tpu_custom_call", output_to_operand_aliasing={{}: (4, {})} | custom-call | flops 1500000000 | bytes 7000000 | tf_op jit(solution)/shard_map/mix/pallas_call | solution.py:269
  42.8 0.1 collective-permute-done.4.block
  42.9 2.3 %mix.13.refs_0_ = f32[72,96,128]{2,1,0:T(8,128)S(1)} custom-call(s32[1]{0:T(128)} %bitcast.4.source, bf16[72,72,128]{2,1,0:T(8,128)(2,1)S(1)} %copy-done, s32[1,128]{1,0:T(1,128)S(1)} %bitcast.15, bf16[9,96,128]{2,1,0:T(8,128)(2,1)S(1)} %collective-permute-done.4.block, f32[72,96,128]{2,1,0:T(8,128)S(1)} %mix.12.refs_0_), custom_call_target="tpu_custom_call", output_to_operand_aliasing={{}: (4, {})} | custom-call | flops 1500000000 | bytes 7000000 | tf_op jit(solution)/shard_map/mix/pallas_call | solution.py:269
  45.2 2.3 %mix.14.refs_0_ = f32[72,96,128]{2,1,0:T(8,128)S(1)} custom-call(s32[1]{0:T(128)} %bitcast.3.source, bf16[72,72,128]{2,1,0:T(8,128)(2,1)S(1)} %copy-done, s32[1,128]{1,0:T(1,128)S(1)} %bitcast.16, bf16[9,96,128]{2,1,0:T(8,128)(2,1)S(1)} %collective-permute-done.3.block, f32[72,96,128]{2,1,0:T(8,128)S(1)} %mix.13.refs_0_), custom_call_target="tpu_custom_call", output_to_operand_aliasing={{}: (4, {})} | custom-call | flops 1500000000 | bytes 7000000 | tf_op jit(solution)/shard_map/mix/pallas_call | solution.py:269
  47.4 0.1 collective-permute-done.2.block
  47.6 3.2 %mix.15 = f32[72,96,128]{2,1,0:T(8,128)} custom-call(s32[1]{0:T(128)} %bitcast.source, bf16[72,72,128]{2,1,0:T(8,128)(2,1)S(1)} %copy-done, s32[1,128]{1,0:T(1,128)S(1)} %bitcast.17, bf16[9,96,128]{2,1,0:T(8,128)(2,1)S(1)} %collective-permute-done.2.block, f32[72,96,128]{2,1,0:T(8,128)S(1)} %mix.14.refs_0_), custom_call_target="tpu_custom_call" | custom-call | flops 1500000000 | bytes 7000000 | tf_op jit(solution)/shard_map/mix/pallas_call | solution.py:269
  (11 shorter events, 0.0 us)
Async XLA Ops:
  0.0 12.8 %copy-start.2 = (f32[9]{0:T(128)S(1)}, f32[9]{0:T(128)}, u32[]{:S(2)}) copy-start(f32[9]{0:T(128)} %rate.3) | copy-start | bytes 112
  4.6 14.1 %collective-permute-start = (bf16[9,96,256]{2,1,0:T(8,128)(2,1)S(1)}, bf16[9,96,256]{2,1,0:T(8,128)(2,1)S(1)}, u32[]{:S(2)}, u32[]{:S(2)}) collective-permute-start(bf16[9,96,256]{2,1,0:T(8,128)(2,1)S(1)} %get-tuple-element.34), channel_id=1, source_target_pairs={{1,2},{2,1},{3,4},{4,3},{5,6},{6,5},{7,8},{8,7},{9,10},{10,9},{11,... | collective-permute-start | bytes 1327112 | tf_op jit(solution)/shard_map/ppermute | solution.py:319
  12.7 6.1 %collective-permute-start.1 = (bf16[9,96,256]{2,1,0:T(8,128)(2,1)S(1)}, bf16[9,96,256]{2,1,0:T(8,128)(2,1)S(1)}, u32[]{:S(2)}, u32[]{:S(2)}) collective-permute-start(bf16[9,96,256]{2,1,0:T(8,128)(2,1)S(1)} %get-tuple-element.35), channel_id=1, source_target_pairs={{0,1},{1,0},{2,3},{3,2},{4,5},{5,4},{6,7},{7,6},{8,9},{9,8},{10,11... | collective-permute-start | bytes 1327112 | tf_op jit(solution)/shard_map/ppermute | solution.py:320
  12.8 16.8 %copy-start = (bf16[72,72,128]{2,1,0:T(8,128)(2,1)S(1)}, bf16[72,72,128]{2,1,0:T(8,128)(2,1)}, u32[]{:S(2)}) copy-start(bf16[72,72,128]{2,1,0:T(8,128)(2,1)} %flux.15) | copy-start | bytes 3981316
  12.8 16.8 %copy-start.1 = (s32[128]{0:T(128)S(1)}, s32[128]{0:T(128)}, u32[]{:S(2)}) copy-start(s32[128]{0:T(128)} %param.15) | copy-start | bytes 1540
  19.4 12.4 %collective-permute-start.8 = (bf16[9,96,128]{2,1,0:T(8,128)(2,1)S(1)}, bf16[9,96,128]{2,1,0:T(8,128)(2,1)S(1)}, u32[]{:S(2)}, u32[]{:S(2)}) collective-permute-start(bf16[9,96,128]{2,1,0:T(8,128)(2,1)S(1)} %get-tuple-element.43), channel_id=1, source_target_pairs={{0,128},{32,160},{64,192},{96,224},{128,0},{160,32},{192,64},{224,... | collective-permute-start | bytes 663560 | tf_op jit(solution)/shard_map/ppermute | solution.py:347
  19.5 14.7 %collective-permute-start.7 = (bf16[9,96,128]{2,1,0:T(8,128)(2,1)S(1)}, bf16[9,96,128]{2,1,0:T(8,128)(2,1)S(1)}, u32[]{:S(2)}, u32[]{:S(2)}) collective-permute-start(bf16[9,96,128]{2,1,0:T(8,128)(2,1)S(1)} %get-tuple-element.42), channel_id=1, source_target_pairs={{0,96},{32,64},{64,32},{96,0},{128,224},{160,192},{192,160},{224,1... | collective-permute-start | bytes 663560 | tf_op jit(solution)/shard_map/ppermute | solution.py:347
  22.6 15.7 %collective-permute-start.6 = (bf16[9,96,128]{2,1,0:T(8,128)(2,1)S(1)}, bf16[9,96,128]{2,1,0:T(8,128)(2,1)S(1)}, u32[]{:S(2)}, u32[]{:S(2)}) collective-permute-start(bf16[9,96,128]{2,1,0:T(8,128)(2,1)S(1)} %get-tuple-element.41), channel_id=1, source_target_pairs={{0,160},{32,128},{64,224},{96,192},{128,32},{160,0},{192,96},{224,... | collective-permute-start | bytes 663560 | tf_op jit(solution)/shard_map/ppermute | solution.py:347
  24.1 16.4 %collective-permute-start.5 = (bf16[9,96,128]{2,1,0:T(8,128)(2,1)S(1)}, bf16[9,96,128]{2,1,0:T(8,128)(2,1)S(1)}, u32[]{:S(2)}, u32[]{:S(2)}) collective-permute-start(bf16[9,96,128]{2,1,0:T(8,128)(2,1)S(1)} %get-tuple-element.40), channel_id=1, source_target_pairs={{0,192},{32,224},{64,128},{96,160},{128,64},{160,96},{192,0},{224,... | collective-permute-start | bytes 663560 | tf_op jit(solution)/shard_map/ppermute | solution.py:347
  25.2 17.7 %collective-permute-start.4 = (bf16[9,96,128]{2,1,0:T(8,128)(2,1)S(1)}, bf16[9,96,128]{2,1,0:T(8,128)(2,1)S(1)}, u32[]{:S(2)}, u32[]{:S(2)}) collective-permute-start(bf16[9,96,128]{2,1,0:T(8,128)(2,1)S(1)} %get-tuple-element.39), channel_id=1, source_target_pairs={{0,224},{32,192},{64,160},{96,128},{128,96},{160,64},{192,32},{224... | collective-permute-start | bytes 663560 | tf_op jit(solution)/shard_map/ppermute | solution.py:347
  31.9 13.3 %collective-permute-start.3 = (bf16[9,96,128]{2,1,0:T(8,128)(2,1)S(1)}, bf16[9,96,128]{2,1,0:T(8,128)(2,1)S(1)}, u32[]{:S(2)}, u32[]{:S(2)}) collective-permute-start(bf16[9,96,128]{2,1,0:T(8,128)(2,1)S(1)} %get-tuple-element.38), channel_id=1, source_target_pairs={{0,32},{32,0},{64,96},{96,64},{128,160},{160,128},{192,224},{224,1... | collective-permute-start | bytes 663560 | tf_op jit(solution)/shard_map/ppermute | solution.py:347
  34.2 13.3 %collective-permute-start.2 = (bf16[9,96,128]{2,1,0:T(8,128)(2,1)S(1)}, bf16[9,96,128]{2,1,0:T(8,128)(2,1)S(1)}, u32[]{:S(2)}, u32[]{:S(2)}) collective-permute-start(bf16[9,96,128]{2,1,0:T(8,128)(2,1)S(1)} %get-tuple-element.37), channel_id=1, source_target_pairs={{0,64},{32,96},{64,0},{96,32},{128,192},{160,224},{192,128},{224,1... | collective-permute-start | bytes 663560 | tf_op jit(solution)/shard_map/ppermute | solution.py:347

commit v4 on v3

--- a/solution.py
+++ b/solution.py
@@ -22,8 +22,8 @@
 SUB = 6
 OUTER = ((0, -2), (0, -1), (1, -2), (6, 2), (7, 1), (7, 2))
 PART = 48
-SENDS = (4, 3, 5, 2, 6, 7, 1)
-ORDER = (0, 4, 3, 5, 6, 7, 1, 2)
+SENDS = (4, 3, 1, 5, 7, 6, 2)
+ORDER = (0, *SENDS)
 BF16 = jnp.bfloat16
 F32 = jnp.float32
 

time: 51.1 us -> 50.7 us (level)
  starting transfers between devices: 20.1 us -> 19.5 us
    ppermute x7, starting transfers between devices: 12 us -> 11.4 us  [body(): lax.ppermute(blocks[turn], 'lev', [(i, i ^ turn) for i in range(PEERS)])]
  transfers between devices with their start and end apart: 9 -> 9, of which waited for: 3 -> 2; matrix products, arithmetic and copies ran while one was open for 0% -> 0% of each run, Pallas kernels for 40% -> 40%
where the time goes in v4:
time: 50.7 us; the launch traced here: 50.5 us
  Pallas kernels  28.8 us (57%)
  starting transfers between devices  19.5 us (38%)
  waiting for transfers between devices  1.99 us (4%)
    pallas_call x8, Pallas kernels, mix(): pl.pallas_call(functools.partial(mix_kernel, first, last), out_shape=jax....  19.1 us
    ppermute x7, starting transfers between devices, body(): lax.ppermute(blocks[turn], 'lev', [(i, i ^ turn) for i in range(PEERS)])  11.4 us
    ppermute x1, starting transfers between devices, body(): far_rows = lax.ppermute(far_rows, 'tile', swaps(1, count))  8.05 us
    pallas_call x1, Pallas kernels, body(): pl.pallas_call(edge_kernel, out_shape=(pltpu.VMEM((LOCAL, BINS, HALF), F3...  4.63 us
    pallas_call x1, Pallas kernels, body(): pl.pallas_call(inner_kernel, out_shape=(pltpu.VMEM((4, LOCAL, BINS, NX),...  4.49 us
    ppermute x1, waiting for transfers between devices, body(): far_rows = lax.ppermute(far_rows, 'tile', swaps(1, count))  1.45 us
  transfers between devices with their start and end apart: 9, of which 2 were waited for; matrix products, arithmetic and copies ran while one was open for 0% of the time, Pallas kernels for 40%

profile of v4, /device:TPU:6, one launch (start us, length us, event | category | flops | bytes accessed | tf_op | source)
XLA Modules:
  0.0 50.5 jit_solution(1760190893785020533)
XLA Ops:
  0.0 4.6 %edge.1 = (f32[9,96,512]{2,1,0:T(8,128)S(1)}, bf16[9,96,256]{2,1,0:T(8,128)(2,1)S(1)}, bf16[9,96,256]{2,1,0:T(8,128)(2,1)S(1)}, bf16[9,96,512]{2,1,0:T(8,128)(2,...) custom-call(f32[9]{0:T(128)} %rate.3, ...), custom_call_target="tpu_custom_call" | custom-call | flops 600000000 | bytes 5000000 | tf_op jit(solution)/shard_map/edge/pallas_call | solution.py:301
  4.6 8.0 %collective-permute-start = (bf16[9,96,256]{2,1,0:T(8,128)(2,1)S(1)}, bf16[9,96,256]{2,1,0:T(8,128)(2,1)S(1)}, u32[]{:S(2)}, u32[]{:S(2)}) collective-permute-start(bf16[9,96,256]{2,1,0:T(8,128)(2,1)S(1)} %get-tuple-element.34), channel_id=1, source_target_pairs={{1,2},{2,1},{3,4},{4,3},{5,6},{6,5},{7,8},{8,7},{9,10},{10,9},{11,... | collective-permute-start | bytes 1327112 | tf_op jit(solution)/shard_map/ppermute | solution.py:319
  12.7 0.1 collective-permute-start.1
  12.8 0.0 copy-start
  12.8 0.0 copy-start.1
  12.8 4.5 %inner.1 = (bf16[4,9,96,128]{3,2,1,0:T(8,128)(2,1)S(1)}, f32[4,9,96,128]{3,2,1,0:T(8,128)S(1)}, f32[6,9,128]{2,1,0:T(8,128)S(1)}) custom-call(f32[9]{0:T(128)S(1)} %copy-done.2, bf16[192,96]{1,0:T(8,128)(2,1)S(1)} %get-tuple-element.25.forward, bf16[96,192]{1,0:T(8,128)(2,1)S(1)} %get-tuple-element.26.inverse, ...), custom_call_target="tpu_custom_call" | custom-call | flops 600000000 | bytes 8000000 | tf_op jit(solution)/shard_map/inner/pallas_call | solution.py:321
  17.3 1.5 %collective-permute-done.far_rows = bf16[9,96,256]{2,1,0:T(8,128)(2,1)S(1)} collective-permute-done((bf16[9,96,256]{2,1,0:T(8,128)(2,1)S(1)}, bf16[9,96,256]{2,1,0:T(8,128)(2,1)S(1)}, u32[]{:S(2)}, u32[]{:S(2)}) %collective-permute-start) | collective-permute-done | bytes 442400 | tf_op jit(solution)/shard_map/ppermute | solution.py:319
  18.8 0.0 collective-permute-done.1.near_rows
  18.8 0.6 %finish.1 = (bf16[9,96,128]{2,1,0:T(8,128)(2,1)S(1)}, bf16[9,96,128]{2,1,0:T(8,128)(2,1)S(1)}, bf16[9,96,128]{2,1,0:T(8,128)(2,1)S(1)}, bf16[9,96,128]{2,1,0:T(8...) custom-call(bf16[4,9,96,128]{3,2,1,0:T(8,128)(2,1)S(1)} %get-tuple-e, ...), custom_call_target="tpu_custom_call" | custom-call | flops 2000000 | bytes 5000000 | tf_op jit(solution)/shard_map/finish/pallas_call | solution.py:335
  19.4 0.1 collective-permute-start.8
  19.5 3.1 %collective-permute-start.7 = (bf16[9,96,128]{2,1,0:T(8,128)(2,1)S(1)}, bf16[9,96,128]{2,1,0:T(8,128)(2,1)S(1)}, u32[]{:S(2)}, u32[]{:S(2)}) collective-permute-start(bf16[9,96,128]{2,1,0:T(8,128)(2,1)S(1)} %get-tuple-element.42), channel_id=1, source_target_pairs={{0,96},{32,64},{64,32},{96,0},{128,224},{160,192},{192,160},{224,1... | collective-permute-start | bytes 663560 | tf_op jit(solution)/shard_map/ppermute | solution.py:347
  22.6 0.1 collective-permute-start.6
  22.7 3.2 %collective-permute-start.5 = (bf16[9,96,128]{2,1,0:T(8,128)(2,1)S(1)}, bf16[9,96,128]{2,1,0:T(8,128)(2,1)S(1)}, u32[]{:S(2)}, u32[]{:S(2)}) collective-permute-start(bf16[9,96,128]{2,1,0:T(8,128)(2,1)S(1)} %get-tuple-element.40), channel_id=1, source_target_pairs={{0,160},{32,128},{64,224},{96,192},{128,32},{160,0},{192,96},{224,... | collective-permute-start | bytes 663560 | tf_op jit(solution)/shard_map/ppermute | solution.py:347
  26.0 2.3 %mix.8.refs_0_ = f32[72,96,128]{2,1,0:T(8,128)S(1)} custom-call(s32[1]{0:T(128)} %bitcast.9.source, bf16[72,72,128]{2,1,0:T(8,128)(2,1)S(1)} %copy-done, s32[1,128]{1,0:T(1,128)S(1)} %bitcast.10, bf16[9,96,128]{2,1,0:T(8,128)(2,1)S(1)} %get-tuple-element.44.block), custom_call_target="tpu_custom_call" | custom-call | flops 1500000000 | bytes 7000000 | tf_op jit(solution)/shard_map/mix/pallas_call | solution.py:269
  28.3 3.2 %collective-permute-start.3 = (bf16[9,96,128]{2,1,0:T(8,128)(2,1)S(1)}, bf16[9,96,128]{2,1,0:T(8,128)(2,1)S(1)}, u32[]{:S(2)}, u32[]{:S(2)}) collective-permute-start(bf16[9,96,128]{2,1,0:T(8,128)(2,1)S(1)} %get-tuple-element.38), channel_id=1, source_target_pairs={{0,192},{32,224},{64,128},{96,160},{128,64},{160,96},{192,0},{224,... | collective-permute-start | bytes 663560 | tf_op jit(solution)/shard_map/ppermute | solution.py:347
  31.5 2.3 %mix.9.refs_0_ = f32[72,96,128]{2,1,0:T(8,128)S(1)} custom-call(s32[1]{0:T(128)} %bitcast.8.source, bf16[72,72,128]{2,1,0:T(8,128)(2,1)S(1)} %copy-done, s32[1,128]{1,0:T(1,128)S(1)} %bitcast.11, bf16[9,96,128]{2,1,0:T(8,128)(2,1)S(1)} %collective-permute-done.8.block, f32[72,96,128]{2,1,0:T(8,128)S(1)} %mix.8.refs_0_), custom_call_target="tpu_custom_call", output_to_operand_aliasing={{}: (4, {})} | custom-call | flops 1500000000 | bytes 7000000 | tf_op jit(solution)/shard_map/mix/pallas_call | solution.py:269
  33.8 1.6 %collective-permute-start.2 = (bf16[9,96,128]{2,1,0:T(8,128)(2,1)S(1)}, bf16[9,96,128]{2,1,0:T(8,128)(2,1)S(1)}, u32[]{:S(2)}, u32[]{:S(2)}) collective-permute-start(bf16[9,96,128]{2,1,0:T(8,128)(2,1)S(1)} %get-tuple-element.37), channel_id=1, source_target_pairs={{0,64},{32,96},{64,0},{96,32},{128,192},{160,224},{192,128},{224,1... | collective-permute-start | bytes 663560 | tf_op jit(solution)/shard_map/ppermute | solution.py:347
  35.4 2.3 %mix.10.refs_0_ = f32[72,96,128]{2,1,0:T(8,128)S(1)} custom-call(s32[1]{0:T(128)} %bitcast.7.source, bf16[72,72,128]{2,1,0:T(8,128)(2,1)S(1)} %copy-done, s32[1,128]{1,0:T(1,128)S(1)} %bitcast.12, bf16[9,96,128]{2,1,0:T(8,128)(2,1)S(1)} %collective-permute-done.7.block, f32[72,96,128]{2,1,0:T(8,128)S(1)} %mix.9.refs_0_), custom_call_target="tpu_custom_call", output_to_operand_aliasing={{}: (4, {})} | custom-call | flops 1500000000 | bytes 7000000 | tf_op jit(solution)/shard_map/mix/pallas_call | solution.py:269
  37.7 2.3 %mix.11.refs_0_ = f32[72,96,128]{2,1,0:T(8,128)S(1)} custom-call(s32[1]{0:T(128)} %bitcast.6.source, bf16[72,72,128]{2,1,0:T(8,128)(2,1)S(1)} %copy-done, s32[1,128]{1,0:T(1,128)S(1)} %bitcast.13, bf16[9,96,128]{2,1,0:T(8,128)(2,1)S(1)} %collective-permute-done.6.block, f32[72,96,128]{2,1,0:T(8,128)S(1)} %mix.10.refs_0_), custom_call_target="tpu_custom_call", output_to_operand_aliasing={{}: (4, {})} | custom-call | flops 1500000000 | bytes 7000000 | tf_op jit(solution)/shard_map/mix/pallas_call | solution.py:269
  40.0 2.3 %mix.12.refs_0_ = f32[72,96,128]{2,1,0:T(8,128)S(1)} custom-call(s32[1]{0:T(128)} %bitcast.5.source, bf16[72,72,128]{2,1,0:T(8,128)(2,1)S(1)} %copy-done, s32[1,128]{1,0:T(1,128)S(1)} %bitcast.14, bf16[9,96,128]{2,1,0:T(8,128)(2,1)S(1)} %collective-permute-done.5.block, f32[72,96,128]{2,1,0:T(8,128)S(1)} %mix.11.refs_0_), custom_call_target="tpu_custom_call", output_to_operand_aliasing={{}: (4, {})} | custom-call | flops 1500000000 | bytes 7000000 | tf_op jit(solution)/shard_map/mix/pallas_call | solution.py:269
  42.2 2.3 %mix.13.refs_0_ = f32[72,96,128]{2,1,0:T(8,128)S(1)} custom-call(s32[1]{0:T(128)} %bitcast.4.source, bf16[72,72,128]{2,1,0:T(8,128)(2,1)S(1)} %copy-done, s32[1,128]{1,0:T(1,128)S(1)} %bitcast.15, bf16[9,96,128]{2,1,0:T(8,128)(2,1)S(1)} %collective-permute-done.4.block, f32[72,96,128]{2,1,0:T(8,128)S(1)} %mix.12.refs_0_), custom_call_target="tpu_custom_call", output_to_operand_aliasing={{}: (4, {})} | custom-call | flops 1500000000 | bytes 7000000 | tf_op jit(solution)/shard_map/mix/pallas_call | solution.py:269
  44.5 2.3 %mix.14.refs_0_ = f32[72,96,128]{2,1,0:T(8,128)S(1)} custom-call(s32[1]{0:T(128)} %bitcast.3.source, bf16[72,72,128]{2,1,0:T(8,128)(2,1)S(1)} %copy-done, s32[1,128]{1,0:T(1,128)S(1)} %bitcast.16, bf16[9,96,128]{2,1,0:T(8,128)(2,1)S(1)} %collective-permute-done.3.block, f32[72,96,128]{2,1,0:T(8,128)S(1)} %mix.13.refs_0_), custom_call_target="tpu_custom_call", output_to_operand_aliasing={{}: (4, {})} | custom-call | flops 1500000000 | bytes 7000000 | tf_op jit(solution)/shard_map/mix/pallas_call | solution.py:269
  46.8 0.5 %collective-permute-done.2.block = bf16[9,96,128]{2,1,0:T(8,128)(2,1)S(1)} collective-permute-done((bf16[9,96,128]{2,1,0:T(8,128)(2,1)S(1)}, bf16[9,96,128]{2,1,0:T(8,128)(2,1)S(1)}, u32[]{:S(2)}, u32[]{:S(2)}) %collective-permute-start.2) | collective-permute-done | bytes 221216 | tf_op jit(solution)/shard_map/ppermute | solution.py:347
  47.3 3.2 %mix.15 = f32[72,96,128]{2,1,0:T(8,128)} custom-call(s32[1]{0:T(128)} %bitcast.source, bf16[72,72,128]{2,1,0:T(8,128)(2,1)S(1)} %copy-done, s32[1,128]{1,0:T(1,128)S(1)} %bitcast.17, bf16[9,96,128]{2,1,0:T(8,128)(2,1)S(1)} %collective-permute-done.2.block, f32[72,96,128]{2,1,0:T(8,128)S(1)} %mix.14.refs_0_), custom_call_target="tpu_custom_call" | custom-call | flops 1500000000 | bytes 7000000 | tf_op jit(solution)/shard_map/mix/pallas_call | solution.py:269
  (11 shorter events, 0.0 us)
Async XLA Ops:
  0.0 12.8 %copy-start.2 = (f32[9]{0:T(128)S(1)}, f32[9]{0:T(128)}, u32[]{:S(2)}) copy-start(f32[9]{0:T(128)} %rate.3) | copy-start | bytes 112
  4.6 14.1 %collective-permute-start = (bf16[9,96,256]{2,1,0:T(8,128)(2,1)S(1)}, bf16[9,96,256]{2,1,0:T(8,128)(2,1)S(1)}, u32[]{:S(2)}, u32[]{:S(2)}) collective-permute-start(bf16[9,96,256]{2,1,0:T(8,128)(2,1)S(1)} %get-tuple-element.34), channel_id=1, source_target_pairs={{1,2},{2,1},{3,4},{4,3},{5,6},{6,5},{7,8},{8,7},{9,10},{10,9},{11,... | collective-permute-start | bytes 1327112 | tf_op jit(solution)/shard_map/ppermute | solution.py:319
  12.7 6.1 %collective-permute-start.1 = (bf16[9,96,256]{2,1,0:T(8,128)(2,1)S(1)}, bf16[9,96,256]{2,1,0:T(8,128)(2,1)S(1)}, u32[]{:S(2)}, u32[]{:S(2)}) collective-permute-start(bf16[9,96,256]{2,1,0:T(8,128)(2,1)S(1)} %get-tuple-element.35), channel_id=1, source_target_pairs={{0,1},{1,0},{2,3},{3,2},{4,5},{5,4},{6,7},{7,6},{8,9},{9,8},{10,11... | collective-permute-start | bytes 1327112 | tf_op jit(solution)/shard_map/ppermute | solution.py:320
  12.8 13.2 %copy-start = (bf16[72,72,128]{2,1,0:T(8,128)(2,1)S(1)}, bf16[72,72,128]{2,1,0:T(8,128)(2,1)}, u32[]{:S(2)}) copy-start(bf16[72,72,128]{2,1,0:T(8,128)(2,1)} %flux.15) | copy-start | bytes 3981316
  12.8 13.2 %copy-start.1 = (s32[128]{0:T(128)S(1)}, s32[128]{0:T(128)}, u32[]{:S(2)}) copy-start(s32[128]{0:T(128)} %param.15) | copy-start | bytes 1540
  19.4 8.9 %collective-permute-start.8 = (bf16[9,96,128]{2,1,0:T(8,128)(2,1)S(1)}, bf16[9,96,128]{2,1,0:T(8,128)(2,1)S(1)}, u32[]{:S(2)}, u32[]{:S(2)}) collective-permute-start(bf16[9,96,128]{2,1,0:T(8,128)(2,1)S(1)} %get-tuple-element.43), channel_id=1, source_target_pairs={{0,128},{32,160},{64,192},{96,224},{128,0},{160,32},{192,64},{224,... | collective-permute-start | bytes 663560 | tf_op jit(solution)/shard_map/ppermute | solution.py:347
  19.5 14.2 %collective-permute-start.7 = (bf16[9,96,128]{2,1,0:T(8,128)(2,1)S(1)}, bf16[9,96,128]{2,1,0:T(8,128)(2,1)S(1)}, u32[]{:S(2)}, u32[]{:S(2)}) collective-permute-start(bf16[9,96,128]{2,1,0:T(8,128)(2,1)S(1)} %get-tuple-element.42), channel_id=1, source_target_pairs={{0,96},{32,64},{64,32},{96,0},{128,224},{160,192},{192,160},{224,1... | collective-permute-start | bytes 663560 | tf_op jit(solution)/shard_map/ppermute | solution.py:347
  22.6 15.1 %collective-permute-start.6 = (bf16[9,96,128]{2,1,0:T(8,128)(2,1)S(1)}, bf16[9,96,128]{2,1,0:T(8,128)(2,1)S(1)}, u32[]{:S(2)}, u32[]{:S(2)}) collective-permute-start(bf16[9,96,128]{2,1,0:T(8,128)(2,1)S(1)} %get-tuple-element.41), channel_id=1, source_target_pairs={{0,32},{32,0},{64,96},{96,64},{128,160},{160,128},{192,224},{224,1... | collective-permute-start | bytes 663560 | tf_op jit(solution)/shard_map/ppermute | solution.py:347
  22.7 17.2 %collective-permute-start.5 = (bf16[9,96,128]{2,1,0:T(8,128)(2,1)S(1)}, bf16[9,96,128]{2,1,0:T(8,128)(2,1)S(1)}, u32[]{:S(2)}, u32[]{:S(2)}) collective-permute-start(bf16[9,96,128]{2,1,0:T(8,128)(2,1)S(1)} %get-tuple-element.40), channel_id=1, source_target_pairs={{0,160},{32,128},{64,224},{96,192},{128,32},{160,0},{192,96},{224,... | collective-permute-start | bytes 663560 | tf_op jit(solution)/shard_map/ppermute | solution.py:347
  26.0 16.2 %collective-permute-start.4 = (bf16[9,96,128]{2,1,0:T(8,128)(2,1)S(1)}, bf16[9,96,128]{2,1,0:T(8,128)(2,1)S(1)}, u32[]{:S(2)}, u32[]{:S(2)}) collective-permute-start(bf16[9,96,128]{2,1,0:T(8,128)(2,1)S(1)} %get-tuple-element.39), channel_id=1, source_target_pairs={{0,224},{32,192},{64,160},{96,128},{128,96},{160,64},{192,32},{224... | collective-permute-start | bytes 663560 | tf_op jit(solution)/shard_map/ppermute | solution.py:347
  28.3 16.2 %collective-permute-start.3 = (bf16[9,96,128]{2,1,0:T(8,128)(2,1)S(1)}, bf16[9,96,128]{2,1,0:T(8,128)(2,1)S(1)}, u32[]{:S(2)}, u32[]{:S(2)}) collective-permute-start(bf16[9,96,128]{2,1,0:T(8,128)(2,1)S(1)} %get-tuple-element.38), channel_id=1, source_target_pairs={{0,192},{32,224},{64,128},{96,160},{128,64},{160,96},{192,0},{224,... | collective-permute-start | bytes 663560 | tf_op jit(solution)/shard_map/ppermute | solution.py:347
  33.8 13.5 %collective-permute-start.2 = (bf16[9,96,128]{2,1,0:T(8,128)(2,1)S(1)}, bf16[9,96,128]{2,1,0:T(8,128)(2,1)S(1)}, u32[]{:S(2)}, u32[]{:S(2)}) collective-permute-start(bf16[9,96,128]{2,1,0:T(8,128)(2,1)S(1)} %get-tuple-element.37), channel_id=1, source_target_pairs={{0,64},{32,96},{64,0},{96,32},{128,192},{160,224},{192,128},{224,1... | collective-permute-start | bytes 663560 | tf_op jit(solution)/shard_map/ppermute | solution.py:347

commit v5 on v4

--- a/solution.py
+++ b/solution.py
@@ -104,7 +104,7 @@
             )
         )
     ]
-    begin(small + group_copies(pairs, sems, 0, (0, 768)))
+    begin(group_copies(pairs, sems, 0, (0, 768)) + small)
     finish_copies(small)
 
     def some(group, carry):
@@ -241,7 +241,7 @@
             to_out(q).start()
         return carry
 
-    lax.fori_loop(0, LEVELS // SUB, some, 0)
+    lax.fori_loop(0, LEVELS // SUB, some, 0, unroll=2)
     if last:
 
         def finished(q, carry):

time: 50.7 us -> 50.8 us (level)
  no operation moved by 1% of the time
where the time goes in v5:
time: 50.8 us; the launch traced here: 50.7 us
  Pallas kernels  28.7 us (56%)
  starting transfers between devices  19.7 us (39%)
  waiting for transfers between devices  1.95 us (4%)
    pallas_call x8, Pallas kernels, mix(): pl.pallas_call(functools.partial(mix_kernel, first, last), out_shape=jax....  18.9 us
    ppermute x7, starting transfers between devices, body(): lax.ppermute(blocks[turn], 'lev', [(i, i ^ turn) for i in range(PEERS)])  11.6 us
    ppermute x1, starting transfers between devices, body(): far_rows = lax.ppermute(far_rows, 'tile', swaps(1, count))  8.05 us
    pallas_call x1, Pallas kernels, body(): pl.pallas_call(edge_kernel, out_shape=(pltpu.VMEM((LOCAL, BINS, HALF), F3...  4.65 us
    pallas_call x1, Pallas kernels, body(): pl.pallas_call(inner_kernel, out_shape=(pltpu.VMEM((4, LOCAL, BINS, NX),...  4.48 us
    ppermute x1, waiting for transfers between devices, body(): far_rows = lax.ppermute(far_rows, 'tile', swaps(1, count))  1.45 us
  transfers between devices with their start and end apart: 9, of which 2 were waited for; matrix products, arithmetic and copies ran while one was open for 0% of the time, Pallas kernels for 40%

profile of v5, /device:TPU:6, one launch (start us, length us, event | category | flops | bytes accessed | tf_op | source)
XLA Modules:
  0.0 50.7 jit_solution(7105472077133443894)
XLA Ops:
  0.0 4.7 %edge.1 = (f32[9,96,512]{2,1,0:T(8,128)S(1)}, bf16[9,96,256]{2,1,0:T(8,128)(2,1)S(1)}, bf16[9,96,256]{2,1,0:T(8,128)(2,1)S(1)}, bf16[9,96,512]{2,1,0:T(8,128)(2,...) custom-call(f32[9]{0:T(128)} %rate.3, ...), custom_call_target="tpu_custom_call" | custom-call | flops 600000000 | bytes 5000000 | tf_op jit(solution)/shard_map/edge/pallas_call | solution.py:301
  4.7 8.0 %collective-permute-start = (bf16[9,96,256]{2,1,0:T(8,128)(2,1)S(1)}, bf16[9,96,256]{2,1,0:T(8,128)(2,1)S(1)}, u32[]{:S(2)}, u32[]{:S(2)}) collective-permute-start(bf16[9,96,256]{2,1,0:T(8,128)(2,1)S(1)} %get-tuple-element.34), channel_id=1, source_target_pairs={{1,2},{2,1},{3,4},{4,3},{5,6},{6,5},{7,8},{8,7},{9,10},{10,9},{11,... | collective-permute-start | bytes 1327112 | tf_op jit(solution)/shard_map/ppermute | solution.py:319
  12.7 0.1 collective-permute-start.1
  12.8 0.0 copy-start
  12.8 0.0 copy-start.1
  12.9 4.5 %inner.1 = (bf16[4,9,96,128]{3,2,1,0:T(8,128)(2,1)S(1)}, f32[4,9,96,128]{3,2,1,0:T(8,128)S(1)}, f32[6,9,128]{2,1,0:T(8,128)S(1)}) custom-call(f32[9]{0:T(128)S(1)} %copy-done.2, bf16[192,96]{1,0:T(8,128)(2,1)S(1)} %get-tuple-element.25.forward, bf16[96,192]{1,0:T(8,128)(2,1)S(1)} %get-tuple-element.26.inverse, ...), custom_call_target="tpu_custom_call" | custom-call | flops 600000000 | bytes 8000000 | tf_op jit(solution)/shard_map/inner/pallas_call | solution.py:321
  17.3 1.5 %collective-permute-done.far_rows = bf16[9,96,256]{2,1,0:T(8,128)(2,1)S(1)} collective-permute-done((bf16[9,96,256]{2,1,0:T(8,128)(2,1)S(1)}, bf16[9,96,256]{2,1,0:T(8,128)(2,1)S(1)}, u32[]{:S(2)}, u32[]{:S(2)}) %collective-permute-start) | collective-permute-done | bytes 442400 | tf_op jit(solution)/shard_map/ppermute | solution.py:319
  18.8 0.0 collective-permute-done.1.near_rows
  18.8 0.6 %finish.1 = (bf16[9,96,128]{2,1,0:T(8,128)(2,1)S(1)}, bf16[9,96,128]{2,1,0:T(8,128)(2,1)S(1)}, bf16[9,96,128]{2,1,0:T(8,128)(2,1)S(1)}, bf16[9,96,128]{2,1,0:T(8...) custom-call(bf16[4,9,96,128]{3,2,1,0:T(8,128)(2,1)S(1)} %get-tuple-e, ...), custom_call_target="tpu_custom_call" | custom-call | flops 2000000 | bytes 5000000 | tf_op jit(solution)/shard_map/finish/pallas_call | solution.py:335
  19.4 0.1 collective-permute-start.8
  19.5 3.1 %collective-permute-start.7 = (bf16[9,96,128]{2,1,0:T(8,128)(2,1)S(1)}, bf16[9,96,128]{2,1,0:T(8,128)(2,1)S(1)}, u32[]{:S(2)}, u32[]{:S(2)}) collective-permute-start(bf16[9,96,128]{2,1,0:T(8,128)(2,1)S(1)} %get-tuple-element.42), channel_id=1, source_target_pairs={{0,96},{32,64},{64,32},{96,0},{128,224},{160,192},{192,160},{224,1... | collective-permute-start | bytes 663560 | tf_op jit(solution)/shard_map/ppermute | solution.py:347
  22.6 0.1 collective-permute-start.6
  22.8 3.2 %collective-permute-start.5 = (bf16[9,96,128]{2,1,0:T(8,128)(2,1)S(1)}, bf16[9,96,128]{2,1,0:T(8,128)(2,1)S(1)}, u32[]{:S(2)}, u32[]{:S(2)}) collective-permute-start(bf16[9,96,128]{2,1,0:T(8,128)(2,1)S(1)} %get-tuple-element.40), channel_id=1, source_target_pairs={{0,160},{32,128},{64,224},{96,192},{128,32},{160,0},{192,96},{224,... | collective-permute-start | bytes 663560 | tf_op jit(solution)/shard_map/ppermute | solution.py:347
  26.0 2.2 %mix.8.refs_0_ = f32[72,96,128]{2,1,0:T(8,128)S(1)} custom-call(s32[1]{0:T(128)} %bitcast.9.source, bf16[72,72,128]{2,1,0:T(8,128)(2,1)S(1)} %copy-done, s32[1,128]{1,0:T(1,128)S(1)} %bitcast.10, bf16[9,96,128]{2,1,0:T(8,128)(2,1)S(1)} %get-tuple-element.44.block), custom_call_target="tpu_custom_call" | custom-call | flops 1500000000 | bytes 7000000 | tf_op jit(solution)/shard_map/mix/pallas_call | solution.py:269
  28.3 3.2 %collective-permute-start.3 = (bf16[9,96,128]{2,1,0:T(8,128)(2,1)S(1)}, bf16[9,96,128]{2,1,0:T(8,128)(2,1)S(1)}, u32[]{:S(2)}, u32[]{:S(2)}) collective-permute-start(bf16[9,96,128]{2,1,0:T(8,128)(2,1)S(1)} %get-tuple-element.38), channel_id=1, source_target_pairs={{0,192},{32,224},{64,128},{96,160},{128,64},{160,96},{192,0},{224,... | collective-permute-start | bytes 663560 | tf_op jit(solution)/shard_map/ppermute | solution.py:347
  31.5 2.2 %mix.9.refs_0_ = f32[72,96,128]{2,1,0:T(8,128)S(1)} custom-call(s32[1]{0:T(128)} %bitcast.8.source, bf16[72,72,128]{2,1,0:T(8,128)(2,1)S(1)} %copy-done, s32[1,128]{1,0:T(1,128)S(1)} %bitcast.11, bf16[9,96,128]{2,1,0:T(8,128)(2,1)S(1)} %collective-permute-done.8.block, f32[72,96,128]{2,1,0:T(8,128)S(1)} %mix.8.refs_0_), custom_call_target="tpu_custom_call", output_to_operand_aliasing={{}: (4, {})} | custom-call | flops 1500000000 | bytes 7000000 | tf_op jit(solution)/shard_map/mix/pallas_call | solution.py:269
  33.7 1.8 %collective-permute-start.2 = (bf16[9,96,128]{2,1,0:T(8,128)(2,1)S(1)}, bf16[9,96,128]{2,1,0:T(8,128)(2,1)S(1)}, u32[]{:S(2)}, u32[]{:S(2)}) collective-permute-start(bf16[9,96,128]{2,1,0:T(8,128)(2,1)S(1)} %get-tuple-element.37), channel_id=1, source_target_pairs={{0,64},{32,96},{64,0},{96,32},{128,192},{160,224},{192,128},{224,1... | collective-permute-start | bytes 663560 | tf_op jit(solution)/shard_map/ppermute | solution.py:347
  35.6 2.2 %mix.10.refs_0_ = f32[72,96,128]{2,1,0:T(8,128)S(1)} custom-call(s32[1]{0:T(128)} %bitcast.7.source, bf16[72,72,128]{2,1,0:T(8,128)(2,1)S(1)} %copy-done, s32[1,128]{1,0:T(1,128)S(1)} %bitcast.12, bf16[9,96,128]{2,1,0:T(8,128)(2,1)S(1)} %collective-permute-done.7.block, f32[72,96,128]{2,1,0:T(8,128)S(1)} %mix.9.refs_0_), custom_call_target="tpu_custom_call", output_to_operand_aliasing={{}: (4, {})} | custom-call | flops 1500000000 | bytes 7000000 | tf_op jit(solution)/shard_map/mix/pallas_call | solution.py:269
  37.8 2.2 %mix.11.refs_0_ = f32[72,96,128]{2,1,0:T(8,128)S(1)} custom-call(s32[1]{0:T(128)} %bitcast.6.source, bf16[72,72,128]{2,1,0:T(8,128)(2,1)S(1)} %copy-done, s32[1,128]{1,0:T(1,128)S(1)} %bitcast.13, bf16[9,96,128]{2,1,0:T(8,128)(2,1)S(1)} %collective-permute-done.6.block, f32[72,96,128]{2,1,0:T(8,128)S(1)} %mix.10.refs_0_), custom_call_target="tpu_custom_call", output_to_operand_aliasing={{}: (4, {})} | custom-call | flops 1500000000 | bytes 7000000 | tf_op jit(solution)/shard_map/mix/pallas_call | solution.py:269
  40.1 2.2 %mix.12.refs_0_ = f32[72,96,128]{2,1,0:T(8,128)S(1)} custom-call(s32[1]{0:T(128)} %bitcast.5.source, bf16[72,72,128]{2,1,0:T(8,128)(2,1)S(1)} %copy-done, s32[1,128]{1,0:T(1,128)S(1)} %bitcast.14, bf16[9,96,128]{2,1,0:T(8,128)(2,1)S(1)} %collective-permute-done.5.block, f32[72,96,128]{2,1,0:T(8,128)S(1)} %mix.11.refs_0_), custom_call_target="tpu_custom_call", output_to_operand_aliasing={{}: (4, {})} | custom-call | flops 1500000000 | bytes 7000000 | tf_op jit(solution)/shard_map/mix/pallas_call | solution.py:269
  42.3 2.2 %mix.13.refs_0_ = f32[72,96,128]{2,1,0:T(8,128)S(1)} custom-call(s32[1]{0:T(128)} %bitcast.4.source, bf16[72,72,128]{2,1,0:T(8,128)(2,1)S(1)} %copy-done, s32[1,128]{1,0:T(1,128)S(1)} %bitcast.15, bf16[9,96,128]{2,1,0:T(8,128)(2,1)S(1)} %collective-permute-done.4.block, f32[72,96,128]{2,1,0:T(8,128)S(1)} %mix.12.refs_0_), custom_call_target="tpu_custom_call", output_to_operand_aliasing={{}: (4, {})} | custom-call | flops 1500000000 | bytes 7000000 | tf_op jit(solution)/shard_map/mix/pallas_call | solution.py:269
  44.6 2.2 %mix.14.refs_0_ = f32[72,96,128]{2,1,0:T(8,128)S(1)} custom-call(s32[1]{0:T(128)} %bitcast.3.source, bf16[72,72,128]{2,1,0:T(8,128)(2,1)S(1)} %copy-done, s32[1,128]{1,0:T(1,128)S(1)} %bitcast.16, bf16[9,96,128]{2,1,0:T(8,128)(2,1)S(1)} %collective-permute-done.3.block, f32[72,96,128]{2,1,0:T(8,128)S(1)} %mix.13.refs_0_), custom_call_target="tpu_custom_call", output_to_operand_aliasing={{}: (4, {})} | custom-call | flops 1500000000 | bytes 7000000 | tf_op jit(solution)/shard_map/mix/pallas_call | solution.py:269
  46.8 0.5 collective-permute-done.2.block
  47.3 3.2 %mix.15 = f32[72,96,128]{2,1,0:T(8,128)} custom-call(s32[1]{0:T(128)} %bitcast.source, bf16[72,72,128]{2,1,0:T(8,128)(2,1)S(1)} %copy-done, s32[1,128]{1,0:T(1,128)S(1)} %bitcast.17, bf16[9,96,128]{2,1,0:T(8,128)(2,1)S(1)} %collective-permute-done.2.block, f32[72,96,128]{2,1,0:T(8,128)S(1)} %mix.14.refs_0_), custom_call_target="tpu_custom_call" | custom-call | flops 1500000000 | bytes 7000000 | tf_op jit(solution)/shard_map/mix/pallas_call | solution.py:269
  (11 shorter events, 0.0 us)
Async XLA Ops:
  0.0 12.8 %copy-start.2 = (f32[9]{0:T(128)S(1)}, f32[9]{0:T(128)}, u32[]{:S(2)}) copy-start(f32[9]{0:T(128)} %rate.3) | copy-start | bytes 112
  4.7 14.1 %collective-permute-start = (bf16[9,96,256]{2,1,0:T(8,128)(2,1)S(1)}, bf16[9,96,256]{2,1,0:T(8,128)(2,1)S(1)}, u32[]{:S(2)}, u32[]{:S(2)}) collective-permute-start(bf16[9,96,256]{2,1,0:T(8,128)(2,1)S(1)} %get-tuple-element.34), channel_id=1, source_target_pairs={{1,2},{2,1},{3,4},{4,3},{5,6},{6,5},{7,8},{8,7},{9,10},{10,9},{11,... | collective-permute-start | bytes 1327112 | tf_op jit(solution)/shard_map/ppermute | solution.py:319
  12.7 6.1 %collective-permute-start.1 = (bf16[9,96,256]{2,1,0:T(8,128)(2,1)S(1)}, bf16[9,96,256]{2,1,0:T(8,128)(2,1)S(1)}, u32[]{:S(2)}, u32[]{:S(2)}) collective-permute-start(bf16[9,96,256]{2,1,0:T(8,128)(2,1)S(1)} %get-tuple-element.35), channel_id=1, source_target_pairs={{0,1},{1,0},{2,3},{3,2},{4,5},{5,4},{6,7},{7,6},{8,9},{9,8},{10,11... | collective-permute-start | bytes 1327112 | tf_op jit(solution)/shard_map/ppermute | solution.py:320
  12.8 13.2 %copy-start = (bf16[72,72,128]{2,1,0:T(8,128)(2,1)S(1)}, bf16[72,72,128]{2,1,0:T(8,128)(2,1)}, u32[]{:S(2)}) copy-start(bf16[72,72,128]{2,1,0:T(8,128)(2,1)} %flux.15) | copy-start | bytes 3981316
  12.8 13.2 %copy-start.1 = (s32[128]{0:T(128)S(1)}, s32[128]{0:T(128)}, u32[]{:S(2)}) copy-start(s32[128]{0:T(128)} %param.15) | copy-start | bytes 1540
  19.4 8.8 %collective-permute-start.8 = (bf16[9,96,128]{2,1,0:T(8,128)(2,1)S(1)}, bf16[9,96,128]{2,1,0:T(8,128)(2,1)S(1)}, u32[]{:S(2)}, u32[]{:S(2)}) collective-permute-start(bf16[9,96,128]{2,1,0:T(8,128)(2,1)S(1)} %get-tuple-element.43), channel_id=1, source_target_pairs={{0,128},{32,160},{64,192},{96,224},{128,0},{160,32},{192,64},{224,... | collective-permute-start | bytes 663560 | tf_op jit(solution)/shard_map/ppermute | solution.py:347
  19.5 14.2 %collective-permute-start.7 = (bf16[9,96,128]{2,1,0:T(8,128)(2,1)S(1)}, bf16[9,96,128]{2,1,0:T(8,128)(2,1)S(1)}, u32[]{:S(2)}, u32[]{:S(2)}) collective-permute-start(bf16[9,96,128]{2,1,0:T(8,128)(2,1)S(1)} %get-tuple-element.42), channel_id=1, source_target_pairs={{0,96},{32,64},{64,32},{96,0},{128,224},{160,192},{192,160},{224,1... | collective-permute-start | bytes 663560 | tf_op jit(solution)/shard_map/ppermute | solution.py:347
  22.6 15.2 %collective-permute-start.6 = (bf16[9,96,128]{2,1,0:T(8,128)(2,1)S(1)}, bf16[9,96,128]{2,1,0:T(8,128)(2,1)S(1)}, u32[]{:S(2)}, u32[]{:S(2)}) collective-permute-start(bf16[9,96,128]{2,1,0:T(8,128)(2,1)S(1)} %get-tuple-element.41), channel_id=1, source_target_pairs={{0,32},{32,0},{64,96},{96,64},{128,160},{160,128},{192,224},{224,1... | collective-permute-start | bytes 663560 | tf_op jit(solution)/shard_map/ppermute | solution.py:347
  22.8 17.3 %collective-permute-start.5 = (bf16[9,96,128]{2,1,0:T(8,128)(2,1)S(1)}, bf16[9,96,128]{2,1,0:T(8,128)(2,1)S(1)}, u32[]{:S(2)}, u32[]{:S(2)}) collective-permute-start(bf16[9,96,128]{2,1,0:T(8,128)(2,1)S(1)} %get-tuple-element.40), channel_id=1, source_target_pairs={{0,160},{32,128},{64,224},{96,192},{128,32},{160,0},{192,96},{224,... | collective-permute-start | bytes 663560 | tf_op jit(solution)/shard_map/ppermute | solution.py:347
  26.0 16.3 %collective-permute-start.4 = (bf16[9,96,128]{2,1,0:T(8,128)(2,1)S(1)}, bf16[9,96,128]{2,1,0:T(8,128)(2,1)S(1)}, u32[]{:S(2)}, u32[]{:S(2)}) collective-permute-start(bf16[9,96,128]{2,1,0:T(8,128)(2,1)S(1)} %get-tuple-element.39), channel_id=1, source_target_pairs={{0,224},{32,192},{64,160},{96,128},{128,96},{160,64},{192,32},{224... | collective-permute-start | bytes 663560 | tf_op jit(solution)/shard_map/ppermute | solution.py:347
  28.3 16.3 %collective-permute-start.3 = (bf16[9,96,128]{2,1,0:T(8,128)(2,1)S(1)}, bf16[9,96,128]{2,1,0:T(8,128)(2,1)S(1)}, u32[]{:S(2)}, u32[]{:S(2)}) collective-permute-start(bf16[9,96,128]{2,1,0:T(8,128)(2,1)S(1)} %get-tuple-element.38), channel_id=1, source_target_pairs={{0,192},{32,224},{64,128},{96,160},{128,64},{160,96},{192,0},{224,... | collective-permute-start | bytes 663560 | tf_op jit(solution)/shard_map/ppermute | solution.py:347
  33.7 13.6 %collective-permute-start.2 = (bf16[9,96,128]{2,1,0:T(8,128)(2,1)S(1)}, bf16[9,96,128]{2,1,0:T(8,128)(2,1)S(1)}, u32[]{:S(2)}, u32[]{:S(2)}) collective-permute-start(bf16[9,96,128]{2,1,0:T(8,128)(2,1)S(1)} %get-tuple-element.37), channel_id=1, source_target_pairs={{0,64},{32,96},{64,0},{96,32},{128,192},{160,224},{192,128},{224,1... | collective-permute-start | bytes 663560 | tf_op jit(solution)/shard_map/ppermute | solution.py:347
